TPU v7x, 256 devices: a whole 4x4x8 slice. The times are simulated.
256 devices in a mesh: gx: 16 (over z_hi, x), gy: 16 (over z_lo, y, core).
Axes of the slice: x: 4, y: 4, z: 8 (z_hi: 4, z_lo: 2; z = z_hi * 2 + z_lo), core: 2. Of those that a mesh axis runs over, the one named last changes fastest.
Arguments:
- facies: int32 [128, 256, 128], P('gx', 'gy'), may hold values from 0 to 7
- source: float32 [128, 256, 128], P('gx', 'gy'), may hold values from -5 to 5
- facies_perm: float32 [8], replicated, may hold values from 0.5 to 5
- facies_store: float32 [8], replicated, may hold values from 0.0002 to 0.001
- well_x: int32 [64], replicated, may hold values from 0 to 127
- well_y: int32 [64], replicated, may hold values from 0 to 255
- well_rate: float32 [64], replicated, may hold values from -2000 to 2000
Outputs:
- pressure: float32 [128, 256, 128], P('gx', 'gy')
All inputs are finite; a program needn't handle non-finite values.
Results may differ from a plain program's by a relative error of at most 0.0003.
Values sent between devices are 32-bit elements; how exact they have to be, the bound alone decides.
A program may use at most 128 MiB of HBM per device.

v0:
```python
import jax
import jax.numpy as jnp
import numpy as np
from jax import lax
from jax.sharding import PartitionSpec as P

BLOCK_X = 64
BLOCK_Y = 64
BLOCK_Z = 16
SWEEPS = 3


RELAX_WEIGHT = 2.0 / 3.0
HIGHEST = lax.Precision.HIGHEST
first_bits = np.array([0, 0, 0, 0, 1, 1, 1, 1], dtype=np.int32)
second_bits = np.array([0, 0, 1, 1, 0, 0, 1, 1], dtype=np.int32)
third_bits = np.array([0, 1, 0, 1, 0, 1, 0, 1], dtype=np.int32)
shift_along_x = np.array([0, 2, -2, 0, 0, 0, 0], dtype=np.int32)
shift_along_y = np.array([0, 0, 0, 2, -2, 0, 0], dtype=np.int32)
shift_along_z = np.array([0, 0, 0, 0, 0, 2, -2], dtype=np.int32)


def with_halo(value, sides, width):
    for axis, dim in sides:
        size, length = (lax.axis_size(axis), value.shape[dim])
        up = [(i, (i + 1) % size) for i in range(size - 1)]
        down = [(j, i) for i, j in up]
        last = lax.slice_in_dim(value, length - width, length, axis=dim)
        initial = lax.slice_in_dim(value, 0, width, axis=dim)
        before = lax.ppermute(last, axis, up)
        after = lax.ppermute(initial, axis, down)
        value = jnp.concatenate([before, value, after], axis=dim)
    return value


def support_of(coords, block_size, parity):
    return parity + 2 * jnp.floor_divide(
        coords + block_size // 2 - block_size * parity, 2 * block_size
    )


def parity_nodes(coords, block_size):
    return jnp.stack([support_of(coords, block_size, 0), support_of(coords, block_size, 1)])


def parity_start(coords, block_size):
    node_ids = parity_nodes(coords, block_size)
    return (node_ids == jnp.floor_divide(coords, block_size)[None]).astype(jnp.float32)


def parity_same(coords, block_size):
    node_here = parity_nodes(coords[:-1], block_size)
    node_next = parity_nodes(coords[1:], block_size)
    return (node_here == node_next).astype(jnp.float32)


def harmonic(left_perm, right_perm):
    return 2.0 * left_perm * right_perm / (left_perm + right_perm)


def face_pad(values_in, dim_id, before):
    widths = [(0, 0), (0, 0), (0, 0)]
    widths[dim_id] = (1, 0) if before else (0, 1)
    return jnp.pad(values_in, widths)


def expand(line_in, dim_id):
    new_shape = [1, 1, 1]
    new_shape[dim_id] = line_in.shape[0]
    return line_in.reshape(new_shape)


def split_faces(values_in, dim_id):
    length = values_in.shape[dim_id]
    below_part = lax.slice_in_dim(values_in, 0, length - 1, axis=dim_id)
    above_part = lax.slice_in_dim(values_in, 1, length, axis=dim_id)
    return (below_part, above_part)


def cut_apply(values_in, storage, trans_all, same_all):
    result = storage * values_in
    for dim_id in range(3):
        trans_face = trans_all[dim_id]
        same_line = expand(same_all[dim_id], dim_id)
        below_part, above_part = split_faces(values_in, dim_id)
        result = result + face_pad(
            trans_face * (below_part - same_line * above_part), dim_id, False
        )
        result = result + face_pad(trans_face * (above_part - same_line * below_part), dim_id, True)
    return result


def rim_terms(values_in, trans_all, same_all):
    result = []
    for dim_id in range(3):
        trans_face = trans_all[dim_id]
        cross_mask = 1.0 - expand(same_all[dim_id], dim_id)
        below_part, above_part = split_faces(values_in, dim_id)
        result.append(face_pad(-trans_face * cross_mask * above_part, dim_id, False))
        result.append(face_pad(-trans_face * cross_mask * below_part, dim_id, True))
    return result


def diagonal_of(storage, trans_all):
    result = storage
    for dim_id in range(3):
        result = (
            result
            + face_pad(trans_all[dim_id], dim_id, False)
            + face_pad(trans_all[dim_id], dim_id, True)
        )
    return result


def lookup(facies, code_table):
    result = jnp.zeros(facies.shape, jnp.float32)
    for code_id in range(code_table.shape[0]):
        result = result + jnp.where(facies == code_id, code_table[code_id], 0.0)
    return result


def flatten_node(index_x, index_y, index_z, counts):
    count_x, count_y, count_z = counts
    flat_ids = (
        jnp.clip(index_x, 0, count_x - 1) * count_y + jnp.clip(index_y, 0, count_y - 1)
    ) * count_z
    return (flat_ids + jnp.clip(index_z, 0, count_z - 1)).astype(jnp.int32)


def tile_indices(anchor_x, anchor_y, counts):
    count_x, count_y, count_z = counts
    row_x = parity_nodes(jnp.reshape(anchor_x, (1,)), BLOCK_X)[first_bits][:, 0]
    row_y = parity_nodes(jnp.reshape(anchor_y, (1,)), BLOCK_Y)[second_bits][:, 0]
    seg_first = jnp.maximum(jnp.arange(count_z + 1, dtype=jnp.int32) * BLOCK_Z - BLOCK_Z // 2, 0)
    row_z = parity_nodes(seg_first, BLOCK_Z)[third_bits]
    row_ids = flatten_node(row_x[:, None], row_y[:, None], row_z, counts)
    col_ids = flatten_node(
        row_x[:, None, None] + jnp.asarray(shift_along_x)[None, :, None],
        row_y[:, None, None] + jnp.asarray(shift_along_y)[None, :, None],
        row_z[:, None, :] + jnp.asarray(shift_along_z)[None, :, None],
        counts,
    )
    entry_ids = row_ids[None, :, None, :] * (count_x * count_y * count_z) + col_ids[:, None, :, :]
    return (entry_ids, row_ids)


def segment_matrix(layers, segment_count):
    seg_of = (jnp.arange(layers, dtype=jnp.int32) + BLOCK_Z // 2) // BLOCK_Z
    return (seg_of[:, None] == jnp.arange(segment_count, dtype=jnp.int32)[None, :]).astype(
        jnp.float32
    )


def solve_coarse(coarse, coarse_rhs):
    factor = jnp.linalg.cholesky(coarse)
    middle = lax.linalg.triangular_solve(factor, coarse_rhs[:, None], left_side=True, lower=True)
    return lax.linalg.triangular_solve(
        factor, middle, left_side=True, lower=True, transpose_a=True
    )[:, 0]


def geometry(coeffs, margin, anchor_x, anchor_y, total_x, total_y):
    coord_x = anchor_x - margin + jnp.arange(coeffs.shape[1], dtype=jnp.int32)
    coord_y = anchor_y - margin + jnp.arange(coeffs.shape[2], dtype=jnp.int32)
    coord_z = jnp.arange(coeffs.shape[3], dtype=jnp.int32)
    inside_x = (coord_x >= 0) & (coord_x < total_x)
    inside_y = (coord_y >= 0) & (coord_y < total_y)
    inside = inside_x[:, None, None] & inside_y[None, :, None]
    perm_safe = jnp.where(inside, coeffs[0], 1.0)
    storage = jnp.where(inside, coeffs[1], 1.0)
    valid_x = (inside_x[:-1] & inside_x[1:]).astype(jnp.float32)
    valid_y = (inside_y[:-1] & inside_y[1:]).astype(jnp.float32)
    trans_x = harmonic(perm_safe[:-1], perm_safe[1:]) * valid_x[:, None, None]
    trans_y = harmonic(perm_safe[:, :-1], perm_safe[:, 1:]) * valid_y[None, :, None]
    trans_z = harmonic(perm_safe[:, :, :-1], perm_safe[:, :, 1:])
    trans_all = (trans_x, trans_y, trans_z)
    same_all = (
        parity_same(coord_x, BLOCK_X)[first_bits],
        parity_same(coord_y, BLOCK_Y)[second_bits],
        parity_same(coord_z, BLOCK_Z)[third_bits],
    )
    starts = (
        parity_start(coord_x, BLOCK_X)[first_bits],
        parity_start(coord_y, BLOCK_Y)[second_bits],
        parity_start(coord_z, BLOCK_Z)[third_bits],
    )
    return (storage, trans_all, diagonal_of(storage, trans_all), same_all, starts)


def initial(geo_set):
    start_x, start_y, start_z = geo_set[4]
    return start_x[:, :, None, None] * start_y[:, None, :, None] * start_z[:, None, None, :]


def smooth(basis_ext, geo_set):
    storage, trans_all, diagonal, same_all, starts = geo_set

    def change_of(values_in, same_x, same_y, same_z):
        return (
            -RELAX_WEIGHT
            * cut_apply(values_in, storage, trans_all, (same_x, same_y, same_z))
            / diagonal
        )

    changes = jax.vmap(change_of)(basis_ext, same_all[0], same_all[1], same_all[2])[:, 1:-1, 1:-1]
    interior = basis_ext[:, 1:-1, 1:-1]
    change_sum = jnp.sum(changes, axis=0)
    return interior + changes - interior * change_sum[None]


def basis_halo(basis_now):
    return with_halo(basis_now, (("gx", 1), ("gy", 2)), 1)


def per_device(facies, source, facies_perm, facies_store, well_x, well_y, well_rate):
    tile_x, tile_y, layers = facies.shape
    devs_x = lax.axis_size("gx")
    devs_y = lax.axis_size("gy")
    total_x = tile_x * devs_x
    total_y = tile_y * devs_y
    anchor_x = lax.axis_index("gx") * tile_x
    anchor_y = lax.axis_index("gy") * tile_y
    coeffs = jnp.stack([lookup(facies, facies_perm), lookup(facies, facies_store)])
    coeff_wide = with_halo(coeffs, (("gx", 1), ("gy", 2)), 1)
    geo_one = geometry(coeff_wide, 1, anchor_x, anchor_y, total_x, total_y)
    basis_now = initial(geo_one)[:, 1:-1, 1:-1]
    for sweep_id in range(SWEEPS):
        basis_now = smooth(basis_halo(basis_now), geo_one)
    basis_now = basis_halo(basis_now)
    storage, trans_all, diagonal, same_all, starts = geo_one

    def terms_of(values_in, same_x, same_y, same_z):
        same_three = (same_x, same_y, same_z)
        return jnp.stack(
            [cut_apply(values_in, storage, trans_all, same_three)]
            + rim_terms(values_in, trans_all, same_three)
        )

    term_stack = jax.vmap(terms_of)(basis_now, same_all[0], same_all[1], same_all[2])[
        :, :, 1:-1, 1:-1
    ]
    interior = basis_now[:, 1:-1, 1:-1]
    count_x = total_x // BLOCK_X
    count_y = total_y // BLOCK_Y
    count_z = layers // BLOCK_Z
    counts = (count_x, count_y, count_z)
    coarse_count = count_x * count_y * count_z
    zmatrix = segment_matrix(layers, count_z + 1)
    gram_local = jnp.einsum("apqz,cspqz->casz", interior, term_stack, precision=HIGHEST)
    gram_local = jnp.einsum("casz,zg->casg", gram_local, zmatrix, precision=HIGHEST)
    cell_x = anchor_x + jnp.arange(tile_x, dtype=jnp.int32)
    cell_y = anchor_y + jnp.arange(tile_y, dtype=jnp.int32)
    hit_x = (well_x[:, None] == cell_x[None, :]).astype(jnp.float32)
    hit_y = (well_y[:, None] == cell_y[None, :]).astype(jnp.float32)
    column = jnp.einsum("w,wx,wy->xy", well_rate, hit_x, hit_y, precision=HIGHEST)
    rhs_fine = source + column[:, :, None] / layers
    rhs_local = jnp.einsum("apqz,pqz->az", interior, rhs_fine, precision=HIGHEST)
    rhs_local = jnp.einsum("az,zg->ag", rhs_local, zmatrix, precision=HIGHEST)
    entry_ids, row_ids = tile_indices(anchor_x, anchor_y, counts)
    local_matrix = (
        jnp.zeros((coarse_count * coarse_count,), jnp.float32)
        .at[entry_ids.reshape(-1)]
        .add(gram_local.reshape(-1))
    )
    local_matrix = local_matrix.reshape(coarse_count, coarse_count)
    local_rhs = (
        jnp.zeros((coarse_count,), jnp.float32).at[row_ids.reshape(-1)].add(rhs_local.reshape(-1))
    )
    coarse, coarse_rhs = lax.psum((local_matrix, local_rhs), ("gx", "gy"))
    coarse_solution = solve_coarse(coarse, coarse_rhs)
    values_at = coarse_solution[row_ids]
    per_layer = jnp.einsum("ag,zg->az", values_at, zmatrix, precision=HIGHEST)
    prolonged = jnp.einsum("apqz,az->pqz", interior, per_layer, precision=HIGHEST)
    prolonged_ext = with_halo(prolonged, (("gx", 0), ("gy", 1)), 1)
    ones_all = (
        jnp.ones((tile_x + 1,), jnp.float32),
        jnp.ones((tile_y + 1,), jnp.float32),
        jnp.ones((layers - 1,), jnp.float32),
    )
    applied = cut_apply(prolonged_ext, storage, trans_all, ones_all)[1:-1, 1:-1]
    return prolonged + RELAX_WEIGHT * (rhs_fine - applied) / diagonal[1:-1, 1:-1]


def solution(mesh):
    in_specs = (P("gx", "gy", None), P("gx", "gy", None), P(), P(), P(), P(), P())
    out_specs = P("gx", "gy", None)
    return jax.shard_map(
        per_device, mesh=mesh, in_specs=in_specs, out_specs=out_specs, check_vma=False
    )
```

profile of v0, /device:TPU:95, one launch (start us, length us, event | category | flops | bytes accessed | tf_op | source)
XLA Modules:
  0.0 359.6 jit_solution(4690114688141937146)
XLA Ops:
  3.6 6.0 %collective-permute-start.4 = (f32[8,1,16,128]{3,0,2,1:T(8,128)S(1)}, f32[8,1,16,128]{3,0,2,1:T(8,128)S(1)}, u32[]{:S(2)}, u32[]{:S(2)}) collective-permute-start(f32[8,1,16,128]{3,0,2,1:T(8,128)S(1)} %get-tuple-element.64), channel_id=1, source_target_pairs={{0,16},{16,32},{32,48},{48,64},{64,80},{80,96},{96,112},{112,128},... | collective-permute-start | bytes 196616 | tf_op jit(solution)/shard_map/ppermute | solution.py:30
  14.8 5.9 %add_bitcast_fusion.1 = (f32[1,8,16,128]{3,2,1,0:T(8,128)S(1)}, pred[8,16,128]{2,1,0:T(8,128)(4,1)S(1)}, pred[8,16,128]{2,1,0:T(8,128)(4,1)S(1)}, pred[8,16,128]...) fusion(f32[]{:T(128)} %bitcast.20, f32[]{:T(128)} %bitcast.19, ...), kind=kLoop, calls=%fused_computation.126 | loop fusion | flops 376832 | bytes 262176 | tf_op jit(solution)/shard_map/stack | solution.py:223
  20.7 5.0 %add_bitcast_fusion = f32[1,8,16,128]{3,2,1,0:T(8,128)S(1)} fusion(pred[8,16,128]{2,1,0:T(8,128)(4,1)S(1)} %get-tuple-element.29, pred[8,16,128]{2,1,0:T(8,128)(4,1)S(1)} %get-tuple-element.28, pred[8,16,128]{2,1,0:T(8,128)(4,1)S(1)} %get-tuple-element.27, pred[8,16,128]{2,1,0:T(8,128)(4,1)S(1)} %get-tuple-element.26, ...), kind=kLoop, calls=%fused_computation.125 | loop fusion | flops 245760 | bytes 196640 | tf_op jit(solution)/shard_map/stack | solution.py:223
  25.8 7.6 %collective-permute-start = (f32[2,1,16,128]{3,2,1,0:T(8,128)S(1)}, f32[2,1,16,128]{3,2,1,0:T(8,128)S(1)}, u32[]{:S(2)}, u32[]{:S(2)}) collective-permute-start(f32[2,1,16,128]{3,2,1,0:T(8,128)S(1)} %get-tuple-element.88), channel_id=1, source_target_pairs={{0,16},{16,32},{32,48},{48,64},{64,80},{80,96},{96,112},{112,128},... | collective-permute-start | bytes 49160 | tf_op jit(solution)/shard_map/ppermute | solution.py:30
  43.6 3.7 %collective-permute-start.2 = (f32[2,10,1,128]{3,2,1,0:T(1,128)S(1)}, f32[2,10,1,128]{3,2,1,0:T(1,128)S(1)}, u32[]{:S(2)}, u32[]{:S(2)}) collective-permute-start(f32[2,10,1,128]{3,2,1,0:T(1,128)S(1)} %get-tuple-element.86), channel_id=1, source_target_pairs={{0,1},{1,2},{2,3},{3,4},{4,5},{5,6},{6,7},{7,8},{8,9},{9,10},{10,1... | collective-permute-start | bytes 30728 | tf_op jit(solution)/shard_map/ppermute | solution.py:30
  50.0 4.4 %collective-permute-done.3 = f32[2,10,1,128]{3,2,1,0:T(1,128)S(1)} collective-permute-done((f32[2,10,1,128]{3,2,1,0:T(1,128)S(1)}, f32[2,10,1,128]{3,2,1,0:T(1,128)S(1)}, u32[]{:S(2)}, u32[]{:S(2)}) %collective-permute-start.3) | collective-permute-done | bytes 10272 | tf_op jit(solution)/shard_map/ppermute | solution.py:31
  60.1 4.9 %collective-permute-done.7 = f32[8,10,1,128]{3,0,2,1:T(8,128)S(1)} collective-permute-done((f32[8,10,1,128]{3,0,2,1:T(8,128)S(1)}, f32[8,10,1,128]{3,0,2,1:T(8,128)S(1)}, u32[]{:S(2)}, u32[]{:S(2)}) %collective-permute-start.7) | collective-permute-done | bytes 40992 | tf_op jit(solution)/shard_map/ppermute | solution.py:31
  66.6 7.9 %collective-permute-start.8 = (f32[8,1,16,128]{3,0,2,1:T(8,128)S(1)}, f32[8,1,16,128]{3,0,2,1:T(8,128)S(1)}, u32[]{:S(2)}, u32[]{:S(2)}) collective-permute-start(f32[8,1,16,128]{3,0,2,1:T(8,128)S(1)} %get-tuple-element.78), channel_id=1, source_target_pairs={{0,16},{16,32},{32,48},{48,64},{64,80},{80,96},{96,112},{112,128},... | collective-permute-start | bytes 196616 | tf_op jit(solution)/shard_map/ppermute | solution.py:30
  77.1 6.6 %collective-permute-done.9 = f32[8,1,16,128]{3,0,2,1:T(8,128)S(1)} collective-permute-done((f32[8,1,16,128]{3,0,2,1:T(8,128)S(1)}, f32[8,1,16,128]{3,0,2,1:T(8,128)S(1)}, u32[]{:S(2)}, u32[]{:S(2)}) %collective-permute-start.9) | collective-permute-done | bytes 65568 | tf_op jit(solution)/shard_map/ppermute | solution.py:31
  89.6 4.8 %collective-permute-done.11 = f32[8,10,1,128]{3,0,2,1:T(8,128)S(1)} collective-permute-done((f32[8,10,1,128]{3,0,2,1:T(8,128)S(1)}, f32[8,10,1,128]{3,0,2,1:T(8,128)S(1)}, u32[]{:S(2)}, u32[]{:S(2)}) %collective-permute-start.11) | collective-permute-done | bytes 40992 | tf_op jit(solution)/shard_map/ppermute | solution.py:31
  101.9 5.3 %collective-permute-done.13 = f32[8,1,16,128]{3,0,2,1:T(8,128)S(1)} collective-permute-done((f32[8,1,16,128]{3,0,2,1:T(8,128)S(1)}, f32[8,1,16,128]{3,0,2,1:T(8,128)S(1)}, u32[]{:S(2)}, u32[]{:S(2)}) %collective-permute-start.13) | collective-permute-done | bytes 65568 | tf_op jit(solution)/shard_map/ppermute | solution.py:31
  119.9 4.5 %copy.37 = f32[8,8,16,128]{2,0,1,3:T(8,128)} copy(f32[8,8,16,128]{3,0,2,1:T(8,128)S(1)} %multiply_subtract_fusion) | data formatting | bytes 1048576 | tf_op jit(solution)/shard_map/sub | solution.py:208
  130.0 10.5 %fusion.64 = f32[128,1,8,1]{2,1,3,0:T(1,128)S(1)} fusion(f32[8,16,128,1]{1,3,0,2:T(1,128)S(1)} %copy.47, f32[8,8,16,128]{2,0,1,3:T(8,128)} %copy.37), kind=kOutput, calls=%fused_computation.356 | convolution fusion | flops 1572864 | bytes 593920 | tf_op jit(solution)/shard_map/apqz,pqz->az/dot_general | solution.py:257
  145.8 4.5 %copy.42 = f32[8,8,16,128,1]{2,0,1,4,3:T(8,128)} copy(f32[8,8,16,128,1]{3,0,2,1,4:T(8,128)S(1)} %bitcast.142) | data formatting | bytes 1048576 | tf_op jit(solution)/shard_map/sub | solution.py:208
  160.2 19.0 %copy.36 = f32[7,8,10,18,128]{3,1,2,0,4:T(8,128)} copy(f32[7,8,10,18,128]{4,1,3,2,0:T(8,128)} %bitcast_dynamic-update-slice_fusion) | data formatting | bytes 10321920 | tf_op jit(solution)/shard_map/vmap()/stack | solution.py:234
  179.1 31.6 %fusion.2 = f32[8,8,7,128]{1,0,2,3:T(8,128)} fusion(f32[8,8,16,128,1]{2,0,1,4,3:T(8,128)} %copy.42, f32[8,7,10,18,128]{3,0,2,1,4:T(8,128)} %bitcast.141), kind=kOutput, calls=%fused_computation.14 | convolution fusion | flops 88080384 | bytes 33783808 | tf_op jit(solution)/shard_map/apqz,cspqz->casz/dot_general | solution.py:249
  214.5 28.8 %scatter_custom_fusion = f32[4096]{0:T(1024)S(1)} fusion(s32[4032]{0:T(1024)} %bitcast.148, f32[4032]{0:T(1024)S(1)} %reshape.1002, f32[]{:T(128)} %constant.405.clone.1), kind=kCustom, calls=%fused_computation.178 | custom fusion | flops 4032 | bytes 16896 | tf_op jit(solution)/shard_map/scatter-add | solution.py:263
  243.4 72.7 %all-reduce.42 = (f32[64,64]{0,1:T(8,128)S(1)}, f32[64]{0:T(128)S(1)}) all-reduce(f32[64,64]{0,1:T(8,128)S(1)} %copy.40, f32[64]{0:T(128)S(1)} %scatter_custom_fusion.1), channel_id=1, replica_groups=mesh['gx'=16,'gy'=16] {'gx','gy'}, use_global_device_ids=true, to_apply=%region_4.5 | all-reduce | flops 4160 | bytes 33280 | tf_op jit(solution)/shard_map/psum | solution.py:269
  316.2 5.8 %cholesky.16 = f32[64,64]{1,0:T(8,128)S(1)} custom-call(f32[64,64]{1,0:T(8,128)S(1)} %fusion.20), custom_call_target="Cholesky" | custom-call | tf_op jit(solution)/shard_map/jit(cholesky)/cholesky | solution.py:155
  323.4 4.9 %custom-call.8 = f32[1,64,64]{1,2,0:T(8,128)S(1)} custom-call(f32[1,64,64]{2,1,0:T(8,128)S(1)} %fusion.17), custom_call_target="InvertDiagBlocksLowerTriangular" | custom-call | tf_op jit(solution)/shard_map/triangular_solve | solution.py:157
  330.3 7.3 %collective-permute-start.20 = (f32[1,16,128]{2,1,0:T(8,128)S(1)}, f32[1,16,128]{2,1,0:T(8,128)S(1)}, u32[]{:S(2)}, u32[]{:S(2)}) collective-permute-start(f32[1,16,128]{2,1,0:T(8,128)S(1)} %get-tuple-element.94), channel_id=1, source_target_pairs={{0,16},{16,32},{32,48},{48,64},{64,80},{80,96},{96,112},{112,128},... | collective-permute-start | bytes 24584 | tf_op jit(solution)/shard_map/ppermute | solution.py:30
  339.6 6.7 %collective-permute-done.21 = f32[1,16,128]{2,1,0:T(8,128)S(1)} collective-permute-done((f32[1,16,128]{2,1,0:T(8,128)S(1)}, f32[1,16,128]{2,1,0:T(8,128)S(1)}, u32[]{:S(2)}, u32[]{:S(2)}) %collective-permute-start.21) | collective-permute-done | bytes 8224 | tf_op jit(solution)/shard_map/ppermute | solution.py:31
  346.3 5.2 %collective-permute-start.22 = (f32[10,1,128]{2,1,0:T(1,128)S(1)}, f32[10,1,128]{2,1,0:T(1,128)S(1)}, u32[]{:S(2)}, u32[]{:S(2)}) collective-permute-start(f32[10,1,128]{2,1,0:T(1,128)S(1)} %get-tuple-element.92), channel_id=1, source_target_pairs={{0,1},{1,2},{2,3},{3,4},{4,5},{5,6},{6,7},{7,8},{8,9},{9,10},{10,1... | collective-permute-start | bytes 15368 | tf_op jit(solution)/shard_map/ppermute | solution.py:30
  353.4 5.1 %collective-permute-done.23 = f32[10,1,128]{2,1,0:T(1,128)S(1)} collective-permute-done((f32[10,1,128]{2,1,0:T(1,128)S(1)}, f32[10,1,128]{2,1,0:T(1,128)S(1)}, u32[]{:S(2)}, u32[]{:S(2)}) %collective-permute-start.23) | collective-permute-done | bytes 5152 | tf_op jit(solution)/shard_map/ppermute | solution.py:31
  (209 shorter events, 89.7 us)
Async XLA Ops:
  3.6 52.0 %collective-permute-start.4 = (f32[8,1,16,128]{3,0,2,1:T(8,128)S(1)}, f32[8,1,16,128]{3,0,2,1:T(8,128)S(1)}, u32[]{:S(2)}, u32[]{:S(2)}) collective-permute-start(f32[8,1,16,128]{3,0,2,1:T(8,128)S(1)} %get-tuple-element.64), channel_id=1, source_target_pairs={{0,16},{16,32},{32,48},{48,64},{64,80},{80,96},{96,112},{112,128},... | collective-permute-start | bytes 196616 | tf_op jit(solution)/shard_map/ppermute | solution.py:30
  9.7 45.9 %collective-permute-start.5 = (f32[8,1,16,128]{3,0,2,1:T(8,128)S(1)}, f32[8,1,16,128]{3,0,2,1:T(8,128)S(1)}, u32[]{:S(2)}, u32[]{:S(2)}) collective-permute-start(f32[8,1,16,128]{3,0,2,1:T(8,128)S(1)} %get-tuple-element.65), channel_id=1, source_target_pairs={{16,0},{32,16},{48,32},{64,48},{80,64},{96,80},{112,96},{128,112},... | collective-permute-start | bytes 196616 | tf_op jit(solution)/shard_map/ppermute | solution.py:31
  25.8 17.7 %collective-permute-start = (f32[2,1,16,128]{3,2,1,0:T(8,128)S(1)}, f32[2,1,16,128]{3,2,1,0:T(8,128)S(1)}, u32[]{:S(2)}, u32[]{:S(2)}) collective-permute-start(f32[2,1,16,128]{3,2,1,0:T(8,128)S(1)} %get-tuple-element.88), channel_id=1, source_target_pairs={{0,16},{16,32},{32,48},{48,64},{64,80},{80,96},{96,112},{112,128},... | collective-permute-start | bytes 49160 | tf_op jit(solution)/shard_map/ppermute | solution.py:30
  33.4 10.1 %collective-permute-start.1 = (f32[2,1,16,128]{3,2,1,0:T(8,128)S(1)}, f32[2,1,16,128]{3,2,1,0:T(8,128)S(1)}, u32[]{:S(2)}, u32[]{:S(2)}) collective-permute-start(f32[2,1,16,128]{3,2,1,0:T(8,128)S(1)} %get-tuple-element.89), channel_id=1, source_target_pairs={{16,0},{32,16},{48,32},{64,48},{80,64},{96,80},{112,96},{128,112},... | collective-permute-start | bytes 49160 | tf_op jit(solution)/shard_map/ppermute | solution.py:31
  43.6 6.4 %collective-permute-start.2 = (f32[2,10,1,128]{3,2,1,0:T(1,128)S(1)}, f32[2,10,1,128]{3,2,1,0:T(1,128)S(1)}, u32[]{:S(2)}, u32[]{:S(2)}) collective-permute-start(f32[2,10,1,128]{3,2,1,0:T(1,128)S(1)} %get-tuple-element.86), channel_id=1, source_target_pairs={{0,1},{1,2},{2,3},{3,4},{4,5},{5,6},{6,7},{7,8},{8,9},{9,10},{10,1... | collective-permute-start | bytes 30728 | tf_op jit(solution)/shard_map/ppermute | solution.py:30
  47.3 7.1 %collective-permute-start.3 = (f32[2,10,1,128]{3,2,1,0:T(1,128)S(1)}, f32[2,10,1,128]{3,2,1,0:T(1,128)S(1)}, u32[]{:S(2)}, u32[]{:S(2)}) collective-permute-start(f32[2,10,1,128]{3,2,1,0:T(1,128)S(1)} %get-tuple-element.87), channel_id=1, source_target_pairs={{1,0},{2,1},{3,2},{4,3},{5,4},{6,5},{7,6},{8,7},{9,8},{10,9},{11,1... | collective-permute-start | bytes 30728 | tf_op jit(solution)/shard_map/ppermute | solution.py:31
  55.6 4.5 %collective-permute-start.6 = (f32[8,10,1,128]{3,0,2,1:T(8,128)S(1)}, f32[8,10,1,128]{3,0,2,1:T(8,128)S(1)}, u32[]{:S(2)}, u32[]{:S(2)}) collective-permute-start(f32[8,10,1,128]{3,0,2,1:T(8,128)S(1)} %get-tuple-element.72), channel_id=1, source_target_pairs={{0,1},{1,2},{2,3},{3,4},{4,5},{5,6},{6,7},{7,8},{8,9},{9,10},{10,1... | collective-permute-start | bytes 122888 | tf_op jit(solution)/shard_map/ppermute | solution.py:30
  57.6 7.4 %collective-permute-start.7 = (f32[8,10,1,128]{3,0,2,1:T(8,128)S(1)}, f32[8,10,1,128]{3,0,2,1:T(8,128)S(1)}, u32[]{:S(2)}, u32[]{:S(2)}) collective-permute-start(f32[8,10,1,128]{3,0,2,1:T(8,128)S(1)} %get-tuple-element.73), channel_id=1, source_target_pairs={{1,0},{2,1},{3,2},{4,3},{5,4},{6,5},{7,6},{8,7},{9,8},{10,9},{11,1... | collective-permute-start | bytes 122888 | tf_op jit(solution)/shard_map/ppermute | solution.py:31
  66.6 10.5 %collective-permute-start.8 = (f32[8,1,16,128]{3,0,2,1:T(8,128)S(1)}, f32[8,1,16,128]{3,0,2,1:T(8,128)S(1)}, u32[]{:S(2)}, u32[]{:S(2)}) collective-permute-start(f32[8,1,16,128]{3,0,2,1:T(8,128)S(1)} %get-tuple-element.78), channel_id=1, source_target_pairs={{0,16},{16,32},{32,48},{48,64},{64,80},{80,96},{96,112},{112,128},... | collective-permute-start | bytes 196616 | tf_op jit(solution)/shard_map/ppermute | solution.py:30
  74.5 9.2 %collective-permute-start.9 = (f32[8,1,16,128]{3,0,2,1:T(8,128)S(1)}, f32[8,1,16,128]{3,0,2,1:T(8,128)S(1)}, u32[]{:S(2)}, u32[]{:S(2)}) collective-permute-start(f32[8,1,16,128]{3,0,2,1:T(8,128)S(1)} %get-tuple-element.79), channel_id=1, source_target_pairs={{16,0},{32,16},{48,32},{64,48},{80,64},{96,80},{112,96},{128,112},... | collective-permute-start | bytes 196616 | tf_op jit(solution)/shard_map/ppermute | solution.py:31
  83.7 5.9 %collective-permute-start.10 = (f32[8,10,1,128]{3,0,2,1:T(8,128)S(1)}, f32[8,10,1,128]{3,0,2,1:T(8,128)S(1)}, u32[]{:S(2)}, u32[]{:S(2)}) collective-permute-start(f32[8,10,1,128]{3,0,2,1:T(8,128)S(1)} %get-tuple-element.70), channel_id=1, source_target_pairs={{0,1},{1,2},{2,3},{3,4},{4,5},{5,6},{6,7},{7,8},{8,9},{9,10},{10,1... | collective-permute-start | bytes 122888 | tf_op jit(solution)/shard_map/ppermute | solution.py:30
  87.0 7.4 %collective-permute-start.11 = (f32[8,10,1,128]{3,0,2,1:T(8,128)S(1)}, f32[8,10,1,128]{3,0,2,1:T(8,128)S(1)}, u32[]{:S(2)}, u32[]{:S(2)}) collective-permute-start(f32[8,10,1,128]{3,0,2,1:T(8,128)S(1)} %get-tuple-element.71), channel_id=1, source_target_pairs={{1,0},{2,1},{3,2},{4,3},{5,4},{6,5},{7,6},{8,7},{9,8},{10,9},{11,1... | collective-permute-start | bytes 122888 | tf_op jit(solution)/shard_map/ppermute | solution.py:31
  96.0 5.9 %collective-permute-start.12 = (f32[8,1,16,128]{3,0,2,1:T(8,128)S(1)}, f32[8,1,16,128]{3,0,2,1:T(8,128)S(1)}, u32[]{:S(2)}, u32[]{:S(2)}) collective-permute-start(f32[8,1,16,128]{3,0,2,1:T(8,128)S(1)} %get-tuple-element.76), channel_id=1, source_target_pairs={{0,16},{16,32},{32,48},{48,64},{64,80},{80,96},{96,112},{112,128},... | collective-permute-start | bytes 196616 | tf_op jit(solution)/shard_map/ppermute | solution.py:30
  97.9 9.2 %collective-permute-start.13 = (f32[8,1,16,128]{3,0,2,1:T(8,128)S(1)}, f32[8,1,16,128]{3,0,2,1:T(8,128)S(1)}, u32[]{:S(2)}, u32[]{:S(2)}) collective-permute-start(f32[8,1,16,128]{3,0,2,1:T(8,128)S(1)} %get-tuple-element.77), channel_id=1, source_target_pairs={{16,0},{32,16},{48,32},{64,48},{80,64},{96,80},{112,96},{128,112},... | collective-permute-start | bytes 196616 | tf_op jit(solution)/shard_map/ppermute | solution.py:31
  107.2 7.2 %collective-permute-start.14 = (f32[8,10,1,128]{3,0,2,1:T(8,128)S(1)}, f32[8,10,1,128]{3,0,2,1:T(8,128)S(1)}, u32[]{:S(2)}, u32[]{:S(2)}) collective-permute-start(f32[8,10,1,128]{3,0,2,1:T(8,128)S(1)} %get-tuple-element.68), channel_id=1, source_target_pairs={{0,1},{1,2},{2,3},{3,4},{4,5},{5,6},{6,7},{7,8},{8,9},{9,10},{10,1... | collective-permute-start | bytes 122888 | tf_op jit(solution)/shard_map/ppermute | solution.py:30
  110.2 7.4 %collective-permute-start.15 = (f32[8,10,1,128]{3,0,2,1:T(8,128)S(1)}, f32[8,10,1,128]{3,0,2,1:T(8,128)S(1)}, u32[]{:S(2)}, u32[]{:S(2)}) collective-permute-start(f32[8,10,1,128]{3,0,2,1:T(8,128)S(1)} %get-tuple-element.69), channel_id=1, source_target_pairs={{1,0},{2,1},{3,2},{4,3},{5,4},{6,5},{7,6},{8,7},{9,8},{10,9},{11,1... | collective-permute-start | bytes 122888 | tf_op jit(solution)/shard_map/ppermute | solution.py:31
  124.4 16.1 %collective-permute-start.16 = (f32[8,1,16,128]{3,0,2,1:T(8,128)S(1)}, f32[8,1,16,128]{3,0,2,1:T(8,128)S(1)}, u32[]{:S(2)}, u32[]{:S(2)}) collective-permute-start(f32[8,1,16,128]{3,0,2,1:T(8,128)S(1)} %get-tuple-element.74), channel_id=1, source_target_pairs={{0,16},{16,32},{32,48},{48,64},{64,80},{80,96},{96,112},{112,128},... | collective-permute-start | bytes 196616 | tf_op jit(solution)/shard_map/ppermute | solution.py:30
  126.3 14.2 %collective-permute-start.17 = (f32[8,1,16,128]{3,0,2,1:T(8,128)S(1)}, f32[8,1,16,128]{3,0,2,1:T(8,128)S(1)}, u32[]{:S(2)}, u32[]{:S(2)}) collective-permute-start(f32[8,1,16,128]{3,0,2,1:T(8,128)S(1)} %get-tuple-element.75), channel_id=1, source_target_pairs={{16,0},{32,16},{48,32},{64,48},{80,64},{96,80},{112,96},{128,112},... | collective-permute-start | bytes 196616 | tf_op jit(solution)/shard_map/ppermute | solution.py:31
  140.5 11.2 %collective-permute-start.18 = (f32[8,10,1,128]{3,0,2,1:T(8,128)S(1)}, f32[8,10,1,128]{3,0,2,1:T(8,128)S(1)}, u32[]{:S(2)}, u32[]{:S(2)}) collective-permute-start(f32[8,10,1,128]{3,0,2,1:T(8,128)S(1)} %get-tuple-element.66), channel_id=1, source_target_pairs={{0,1},{1,2},{2,3},{3,4},{4,5},{5,6},{6,7},{7,8},{8,9},{9,10},{10,1... | collective-permute-start | bytes 122888 | tf_op jit(solution)/shard_map/ppermute | solution.py:30
  143.6 8.1 %collective-permute-start.19 = (f32[8,10,1,128]{3,0,2,1:T(8,128)S(1)}, f32[8,10,1,128]{3,0,2,1:T(8,128)S(1)}, u32[]{:S(2)}, u32[]{:S(2)}) collective-permute-start(f32[8,10,1,128]{3,0,2,1:T(8,128)S(1)} %get-tuple-element.67), channel_id=1, source_target_pairs={{1,0},{2,1},{3,2},{4,3},{5,4},{6,5},{7,6},{8,7},{9,8},{10,9},{11,1... | collective-permute-start | bytes 122888 | tf_op jit(solution)/shard_map/ppermute | solution.py:31
  330.3 9.3 %collective-permute-start.20 = (f32[1,16,128]{2,1,0:T(8,128)S(1)}, f32[1,16,128]{2,1,0:T(8,128)S(1)}, u32[]{:S(2)}, u32[]{:S(2)}) collective-permute-start(f32[1,16,128]{2,1,0:T(8,128)S(1)} %get-tuple-element.94), channel_id=1, source_target_pairs={{0,16},{16,32},{32,48},{48,64},{64,80},{80,96},{96,112},{112,128},... | collective-permute-start | bytes 24584 | tf_op jit(solution)/shard_map/ppermute | solution.py:30
  337.6 8.6 %collective-permute-start.21 = (f32[1,16,128]{2,1,0:T(8,128)S(1)}, f32[1,16,128]{2,1,0:T(8,128)S(1)}, u32[]{:S(2)}, u32[]{:S(2)}) collective-permute-start(f32[1,16,128]{2,1,0:T(8,128)S(1)} %get-tuple-element.95), channel_id=1, source_target_pairs={{16,0},{32,16},{48,32},{64,48},{80,64},{96,80},{112,96},{128,112},... | collective-permute-start | bytes 24584 | tf_op jit(solution)/shard_map/ppermute | solution.py:31
  346.3 7.1 %collective-permute-start.22 = (f32[10,1,128]{2,1,0:T(1,128)S(1)}, f32[10,1,128]{2,1,0:T(1,128)S(1)}, u32[]{:S(2)}, u32[]{:S(2)}) collective-permute-start(f32[10,1,128]{2,1,0:T(1,128)S(1)} %get-tuple-element.92), channel_id=1, source_target_pairs={{0,1},{1,2},{2,3},{3,4},{4,5},{5,6},{6,7},{7,8},{8,9},{9,10},{10,1... | collective-permute-start | bytes 15368 | tf_op jit(solution)/shard_map/ppermute | solution.py:30
  351.5 7.0 %collective-permute-start.23 = (f32[10,1,128]{2,1,0:T(1,128)S(1)}, f32[10,1,128]{2,1,0:T(1,128)S(1)}, u32[]{:S(2)}, u32[]{:S(2)}) collective-permute-start(f32[10,1,128]{2,1,0:T(1,128)S(1)} %get-tuple-element.93), channel_id=1, source_target_pairs={{1,0},{2,1},{3,2},{4,3},{5,4},{6,5},{7,6},{8,7},{9,8},{10,9},{11,1... | collective-permute-start | bytes 15368 | tf_op jit(solution)/shard_map/ppermute | solution.py:31
  (14 other events, 767.3 us)
where the time goes:
time: 361 us; the launch traced here: 360 us
  starting transfers between devices  79.7 us (22%)
  blocking collectives  72.7 us (20%)
  other arithmetic  71.4 us (20%)
  local copies, waits for them, and re-layouts  49.7 us (14%)
  matrix products  44 us (12%)
  waiting for transfers between devices  41 us (11%)
    psum x1, blocking collectives, per_device(): coarse, coarse_rhs = lax.psum((local_matrix, local_rhs), ('gx', 'gy'))  72.7 us
    ppermute x12, starting transfers between devices, with_halo(): before = lax.ppermute(last, axis, up)  53 us
    ppermute x12, waiting for transfers between devices, with_halo(): after = lax.ppermute(initial, axis, down)  41 us
    dot_general x1, matrix products, per_device(): jnp.einsum('apqz,cspqz->casz', interior, term_stack, precision=HIGHEST)  31.6 us
    scatter-add x1, other arithmetic, per_device(): local_matrix = jnp.zeros((coarse_count * coarse_count,), jnp.float32).at[...  28.8 us
    ppermute x12, starting transfers between devices, with_halo(): after = lax.ppermute(initial, axis, down)  26.7 us
    another operation x2, local copies, waits for them, and re-layouts, terms_of(): jnp.stack([cut_apply(values_in, storage, trans_all, same_three)] + rim_te...  20.1 us
    another operation x2, other arithmetic, per_device(): jnp.stack([lookup(facies, facies_perm), lookup(facies, facies_store)])  11 us
  transfers between devices with their start and end apart: 24, of which 8 were waited for; matrix products, arithmetic and copies ran while one was open for 13% of the time, Pallas kernels for 0%

commit v1 on v0

v1 whole, which is shorter than its diff:
```python
import functools

import jax
import jax.numpy as jnp
from jax import lax
from jax.experimental import pallas as pl
from jax.experimental.pallas import tpu as pltpu
from jax.sharding import PartitionSpec as P

GRID_X, GRID_Y, CELLS_Z = 128, 256, 128
BLOCK_X, BLOCK_Y, BLOCK_Z = 64, 64, 16
FACIES = 8
WELLS = 64
RELAX = 2.0 / 3.0

TX, TY = 8, 16
HX, HY = 4, 8
EX, EY = TX + 2 * HX, TY + 2 * HY
DX, DY = 16, 16
MESH = pl.DeviceIdType.MESH
F32 = jnp.float32

COLORS = [(c >> 2 & 1, c >> 1 & 1, c & 1) for c in range(8)]
SLOT = [4 * i + j + 8 * k for i, j, k in COLORS]
RHS_SLOT = 2


def roll(value, shift):
    return pltpu.roll(value, shift % 128, 1)


def iota(dim):
    return lax.broadcasted_iota(jnp.int32, (8, 128), dim)


def flag(cond):
    return jnp.where(cond, 1.0, 0.0).astype(F32)


def same_xy(coord, parity, block):
    return flag((coord + 1 + block // 2 - block * parity + 4 * block) % (2 * block) != 0)


def same_z(coord, parity):
    return flag((coord + 1 + BLOCK_Z // 2 - BLOCK_Z * parity + 2 * BLOCK_Z) % (2 * BLOCK_Z) != 0)


def inside(coord, total):
    return (coord >= 0) & (coord < total)


def kernel(
    facies_ref, source_ref, perm_ref, store_ref, wx_ref, wy_ref, wr_ref, out_ref,
    fac, hperm, stor, coef, trans, wdiag, va, vb, bv, rhs, wide, stage1, stage2, val, prol,
    mine, half, hsend, hrecv, xsend, xrecv, ysend, yrecv,
):
    gx = lax.axis_index("gx")
    gy = lax.axis_index("gy")
    ax, ay = gx * TX, gy * TY
    lane, sub = iota(1), iota(0)

    barrier = pltpu.get_barrier_semaphore()
    partners = [((gx + d) % DX, gy) for d in range(1, DX)]
    partners += [(gx, (gy + d) % DY) for d in range(1, DY)]
    corners = [((gx + i) % DX, (gy + j) % DY) for i in (1, DX - 1) for j in (1, DY - 1)]
    for who in partners + corners:
        pl.semaphore_signal(barrier, inc=1, device_id=who, device_id_type=MESH)
    pl.semaphore_wait(barrier, len(partners) + 4)

    copies = []
    n = 0
    for dx in (-1, 0, 1):
        for dy in (-1, 0, 1):
            if dx == 0 and dy == 0:
                continue
            sx = {1: (TX - HX, HX), -1: (0, HX), 0: (0, TX)}[dx]
            sy = {1: (TY - HY, HY), -1: (0, HY), 0: (0, TY)}[dy]
            tx = {1: 0, -1: HX + TX, 0: HX}[dx]
            ty = {1: 0, -1: HY + TY, 0: HY}[dy]
            copies.append(
                pltpu.make_async_remote_copy(
                    src_ref=facies_ref.at[pl.ds(sx[0], sx[1]), pl.ds(sy[0], sy[1])],
                    dst_ref=fac.at[pl.ds(tx, sx[1]), pl.ds(ty, sy[1])],
                    send_sem=hsend.at[n],
                    recv_sem=hrecv.at[n],
                    device_id=((gx + dx + DX) % DX, (gy + dy + DY) % DY),
                    device_id_type=MESH,
                )
            )
            n += 1
    for copy in copies:
        copy.start()

    well_x = wx_ref[...]
    well_y = wy_ref[...]
    well_r = wr_ref[...]
    sub64 = lax.broadcasted_iota(jnp.int32, (8, WELLS), 0)
    for j in range(2):
        hit_y = jnp.where(sub64 + (ay + 8 * j) == well_y, well_r, 0.0)
        for x in range(TX):
            part = jnp.where(well_x == ax + x, hit_y, 0.0)
            column = jnp.sum(part, axis=1, keepdims=True)
            rhs[x, 8 * j : 8 * j + 8, :] = source_ref[x, 8 * j : 8 * j + 8, :] + column / CELLS_Z

    def start_plane(x, _):
        gxe = ax - HX + x
        for t in range(4):
            row = ay - HY + 8 * t + sub
            for c, (i, j, k) in enumerate(COLORS):
                hit = inside(row, GRID_Y) & ((row // BLOCK_Y) % 2 == j) & ((lane // BLOCK_Z) % 2 == k)
                hitx = inside(gxe, GRID_X) & ((gxe + 2 * BLOCK_X) // BLOCK_X % 2 == i)
                va[c, x, 8 * t : 8 * t + 8, :] = flag(hit) * flag(hitx)
        return 0

    lax.fori_loop(0, EX, start_plane, 0)

    fac[HX : HX + TX, HY : HY + TY, :] = facies_ref[...]
    for copy in copies:
        copy.wait()

    half_inv = [0.5 / jnp.full((8, 128), perm_ref[f], F32) for f in range(FACIES)]
    store_at = [jnp.full((8, 128), store_ref[f], F32) for f in range(FACIES)]

    def pick(code, table):
        bits = [(code // (1 << b)) % 2 == 1 for b in range(3)]
        for b in range(3):
            table = [jnp.where(bits[b], hi, lo) for lo, hi in zip(table[::2], table[1::2])]
        return table[0]

    def lookup_plane(x, _):
        for t in range(4):
            code = fac[x, 8 * t : 8 * t + 8, :]
            hperm[x, 8 * t : 8 * t + 8, :] = pick(code, half_inv)
            stor[x, 8 * t : 8 * t + 8, :] = pick(code, store_at)
        return 0

    lax.fori_loop(0, EX, lookup_plane, 0)

    last_z = flag(lane < CELLS_Z - 1)

    def coef_plane(x, _):
        gxe = ax - HX + x
        ok_m = flag(inside(gxe - 1, GRID_X) & inside(gxe, GRID_X))
        ok_p = flag(inside(gxe, GRID_X) & inside(gxe + 1, GRID_X))
        for t in range(3):
            r = 4 + 8 * t
            h = hperm[x, r : r + 8, :]
            row = ay - HY + r + sub
            row_m = flag(inside(row - 1, GRID_Y) & inside(row, GRID_Y))
            row_p = flag(inside(row, GRID_Y) & inside(row + 1, GRID_Y))
            txm = ok_m / (h + hperm[x - 1, r : r + 8, :])
            txp = ok_p / (h + hperm[x + 1, r : r + 8, :])
            tym = row_m / (h + hperm[x, r - 1 : r + 7, :])
            typ = row_p / (h + hperm[x, r + 1 : r + 9, :])
            tzp = last_z / (h + roll(h, -1))
            tzm = roll(tzp, 1)
            diag = stor[x, r : r + 8, :] + txm + txp + tym + typ + tzm + tzp
            w = RELAX / diag
            wdiag[x, r : r + 8, :] = w
            for n, value in enumerate((txm, txp, tym, typ, tzm, tzp)):
                trans[n, x, r : r + 8, :] = value
            wxm, wxp, wym, wyp, wzm, wzp = [w * v for v in (txm, txp, tym, typ, tzm, tzp)]
            a = 8 * t
            for p in range(2):
                coef[p, x, a : a + 8, :] = wxm * same_xy(gxe - 1, p, BLOCK_X)
                coef[2 + p, x, a : a + 8, :] = wxp * same_xy(gxe, p, BLOCK_X)
                coef[4 + p, x, a : a + 8, :] = wym * same_xy(row - 1, p, BLOCK_Y)
                coef[6 + p, x, a : a + 8, :] = wyp * same_xy(row, p, BLOCK_Y)
                coef[8 + p, x, a : a + 8, :] = wzm * same_z(lane - 1, p)
                coef[10 + p, x, a : a + 8, :] = wzp * same_z(lane, p)
        return 0

    lax.fori_loop(1, EX - 1, coef_plane, 0)

    def sweep(src, dst, low):
        def plane(x, _):
            for t in range(3):
                r, a = 4 + 8 * t, 8 * t
                k = [coef[n, x, a : a + 8, :] for n in range(12)]
                old, new = [], []
                for c, (px, py, pz) in enumerate(COLORS):
                    v = src[c, x, r : r + 8, :]
                    q = k[px] * src[c, x - 1, r : r + 8, :] + k[2 + px] * src[c, x + 1, r : r + 8, :]
                    q += k[4 + py] * src[c, x, r - 1 : r + 7, :] + k[6 + py] * src[c, x, r + 1 : r + 9, :]
                    q += k[8 + pz] * roll(v, 1) + k[10 + pz] * roll(v, -1)
                    old.append(v)
                    new.append(q)
                total = functools.reduce(jnp.add, new) - RELAX * functools.reduce(jnp.add, old)
                keep = (1.0 - RELAX) - total
                for c in range(8):
                    dst[c, x, r : r + 8, :] = new[c] + old[c] * keep
            return 0

        lax.fori_loop(low, EX - low, plane, 0)

    sweep(va, vb, 1)
    sweep(vb, va, 2)
    sweep(va, vb, 3)
    basis = vb

    def apply_plane(x, _):
        for t in range(2):
            r = HY + 8 * t
            row = ay + 8 * t + sub
            k = [trans[n, x, r : r + 8, :] for n in range(6)]
            s = stor[x, r : r + 8, :]
            ym = [same_xy(row - 1, p, BLOCK_Y) for p in range(2)]
            yp = [same_xy(row, p, BLOCK_Y) for p in range(2)]
            zm = [same_z(lane - 1, p) for p in range(2)]
            zp = [same_z(lane, p) for p in range(2)]
            for c, (px, py, pz) in enumerate(COLORS):
                v = basis[c, x, r : r + 8, :]
                q = s * v
                q += k[0] * (v - basis[c, x - 1, r : r + 8, :]) + k[1] * (v - basis[c, x + 1, r : r + 8, :])
                q += k[2] * (v - ym[py] * basis[c, x, r - 1 : r + 7, :])
                q += k[3] * (v - yp[py] * basis[c, x, r + 1 : r + 9, :])
                q += k[4] * (v - zm[pz] * roll(v, 1)) + k[5] * (v - zp[pz] * roll(v, -1))
                bv[c, x - HX, 8 * t : 8 * t + 8, :] = q
        return 0

    lax.fori_loop(HX, HX + TX, apply_plane, 0)

    pairs = [(a, c) for a in range(8) for c in range(a, 8)]
    for group in (pairs[:15], pairs[15:30], pairs[30:]):
        rows = sorted({a for a, _ in group})
        cols = sorted({c for _, c in group})
        last = group is not None and group[-1] == (7, 7)

        def gather(x, acc, group=group, rows=rows, cols=cols, last=last):
            acc = list(acc)
            for t in range(2):
                left = {a: basis[a, x + HX, HY + 8 * t : HY + 8 * t + 8, :] for a in (range(8) if last else rows)}
                right = {c: bv[c, x, 8 * t : 8 * t + 8, :] for c in cols}
                for n, (a, c) in enumerate(group):
                    acc[n] = acc[n] + left[a] * right[c]
                if last:
                    load = rhs[x, 8 * t : 8 * t + 8, :]
                    for a in range(8):
                        acc[len(group) + a] = acc[len(group) + a] + left[a] * load
            return tuple(acc)

        count = len(group) + (8 if last else 0)
        acc = lax.fori_loop(0, TX, gather, tuple(jnp.zeros((8, 128), F32) for _ in range(count)))
        for n, (a, c) in enumerate(group):
            line = jnp.sum(acc[n], axis=0, keepdims=True)
            wide[c, a : a + 1, :] = line
            if a != c:
                wide[a, c : c + 1, :] = line
        if last:
            for a in range(8):
                wide[8, a : a + 1, :] = jnp.sum(acc[len(group) + a], axis=0, keepdims=True)

    packed = jnp.zeros((8, 128), F32)
    for n in range(9):
        line = wide[n]
        for step in (1, 2, 4, 8):
            line = line + roll(line, -step)
        line = jnp.where(lane % 16 == 8, line, 0.0)
        packed = packed + roll(line, 8 + (SLOT[n] if n < 8 else RHS_SLOT))

    def exchange(src, slots, send, recv, axis):
        me = gx if axis == 0 else gy
        size = DX if axis == 0 else DY
        sent = []
        for d in range(1, size):
            to = ((gx + d) % DX, gy) if axis == 0 else (gx, (gy + d) % DY)
            copy = pltpu.make_async_remote_copy(
                src_ref=src, dst_ref=slots.at[me], send_sem=send.at[d], recv_sem=recv.at[d],
                device_id=to, device_id_type=MESH,
            )
            copy.start()
            sent.append(copy)
        slots[me] = src[...]
        for copy in sent:
            copy.wait()

    def tree(items):
        while len(items) > 1:
            items = [a + b for a, b in zip(items[::2], items[1::2])] + (items[-1:] if len(items) % 2 else [])
        return items[0]

    mine[...] = packed
    exchange(mine, stage1, xsend, xrecv, 0)
    half[...] = tree([stage1[n] for n in range(DX)])
    exchange(half, stage2, ysend, yrecv, 1)
    sa = tree([stage2[n] for n in range(0, 6)])
    sb = tree([stage2[n] for n in range(6, 10)])
    sc = tree([stage2[n] for n in range(10, 16)])

    pair_j = lane % 4
    low = pair_j < 2
    zero = jnp.zeros((8, 128), F32)

    def put(j0=zero, j1=zero, j2=zero, j3=zero):
        first = jnp.where(pair_j == 0, j0, jnp.where(pair_j == 1, j1, 0.0))
        second = jnp.where(pair_j == 0, j2, jnp.where(pair_j == 1, j3, 0.0))
        return first + roll(second, 2)

    line_of = [
        put(sa, sa),
        put(sa, sa + sb, sb),
        put(zero, sb, sb + sc, sc),
        put(zero, zero, sc, sc),
    ]
    load_of = [sa, sa + sb, sb + sc, sc]
    group = lane // 16
    used = lane % 16 < 8
    even = sub % 2 == 0
    on = used & (group == sub)
    above = used & (group == sub + 1)
    below = used & (group == sub - 1)
    matrix = []
    for ij in range(8):
        i, j = ij // 4, ij % 4
        e = 4 * i + 2 * (j % 2)
        base = line_of[j]
        turns = {s: roll(base, -s) for s in (8, 16, 24)}
        turns[0] = base
        be = {s: jnp.broadcast_to(v[e : e + 1, :], (8, 128)) for s, v in turns.items()}
        bo = {s: jnp.broadcast_to(v[e + 1 : e + 2, :], (8, 128)) for s, v in turns.items()}
        diag_part = jnp.where(even, be[0] + be[16], bo[8] + bo[24])
        up = jnp.where(even, be[8], bo[0])
        down = jnp.where(even, be[24], bo[16])
        block = jnp.where(on, diag_part, jnp.where(above, up, jnp.where(below, down, 0.0)))
        load = jnp.where(lane % 16 == RHS_SLOT, load_of[j], 0.0)
        load = load + roll(load, -16)
        le = jnp.broadcast_to(load[e : e + 1, :], (8, 128))
        lo = jnp.broadcast_to(load[e + 1 : e + 2, :], (8, 128))
        load = jnp.where((group == sub) & (lane % 16 == RHS_SLOT), jnp.where(even, le, lo), 0.0)
        load = jnp.sum(load, axis=1, keepdims=True)
        matrix.append(jnp.where(lane == 8, load, block))

    for kk in range(8):
        for ij in range(8):
            at = 16 * kk + ij
            columns = [m[:, at : at + 1] for m in matrix]
            row = jnp.broadcast_to(matrix[ij][kk : kk + 1, :], (8, 128))
            pivot = jnp.broadcast_to(columns[ij][kk : kk + 1, :], (8, 1))
            row = row / pivot
            for n in range(8):
                update = matrix[n] - columns[n] * row
                if n == ij:
                    update = jnp.where(sub == kk, row, update)
                matrix[n] = update

    node_k = [2 * ((lane + BLOCK_Z // 2) // (2 * BLOCK_Z)),
              2 * ((lane + BLOCK_Z // 2 + BLOCK_Z) // (2 * BLOCK_Z)) - 1]
    for ij in range(8):
        u = matrix[ij][:, 8:9]
        for p in range(2):
            line = jnp.sum(jnp.where(node_k[p] == sub, u, 0.0), axis=0, keepdims=True)
            val[p, ij : ij + 1, :] = line

    def node_row(px, py, pz, tile):
        first = tile * TY
        j = py + 2 * ((first + BLOCK_Y // 2 - BLOCK_Y * py + 4 * BLOCK_Y) // (2 * BLOCK_Y) - 2)
        j = jnp.clip(j, 0, 3)
        return val[pz, pl.ds(4 * px + j, 1), :]

    for t in range(4):
        tile = gy + (-1, 0, 0, 1)[t]
        weights = [jnp.broadcast_to(node_row(px, py, pz, tile), (8, 128)) for px, py, pz in COLORS]

        def prolong(x, _, t=t, weights=weights):
            prol[x, 8 * t : 8 * t + 8, :] = functools.reduce(
                jnp.add, [weights[c] * basis[c, x, 8 * t : 8 * t + 8, :] for c in range(8)]
            )
            return 0

        lax.fori_loop(HX - 1, HX + TX + 1, prolong, 0)

    def finish(x, _):
        for t in range(2):
            r = HY + 8 * t
            v = prol[x, r : r + 8, :]
            k = [trans[n, x, r : r + 8, :] for n in range(6)]
            q = stor[x, r : r + 8, :] * v
            q += k[0] * (v - prol[x - 1, r : r + 8, :]) + k[1] * (v - prol[x + 1, r : r + 8, :])
            q += k[2] * (v - prol[x, r - 1 : r + 7, :]) + k[3] * (v - prol[x, r + 1 : r + 9, :])
            q += k[4] * (v - roll(v, 1)) + k[5] * (v - roll(v, -1))
            load = rhs[x - HX, 8 * t : 8 * t + 8, :]
            out_ref[x - HX, 8 * t : 8 * t + 8, :] = v + wdiag[x, r : r + 8, :] * (load - q)
        return 0

    lax.fori_loop(HX, HX + TX, finish, 0)


def per_device(facies, source, facies_perm, facies_store, well_x, well_y, well_rate):
    vmem = pl.BlockSpec(memory_space=pltpu.VMEM)
    smem = pl.BlockSpec(memory_space=pltpu.SMEM)
    field = pltpu.VMEM((EX, EY, 128), F32)
    colors = pltpu.VMEM((8, EX, EY, 128), F32)
    return pl.pallas_call(
        kernel,
        out_shape=jax.ShapeDtypeStruct((TX, TY, CELLS_Z), F32),
        in_specs=[vmem, vmem, smem, smem, vmem, vmem, vmem],
        out_specs=vmem,
        scratch_shapes=[
            pltpu.VMEM((EX, EY, 128), jnp.int32),
            field,
            field,
            pltpu.VMEM((12, EX, 24, 128), F32),
            pltpu.VMEM((6, EX, EY, 128), F32),
            field,
            colors,
            colors,
            pltpu.VMEM((8, TX, TY, 128), F32),
            pltpu.VMEM((TX, TY, 128), F32),
            pltpu.VMEM((9, 8, 128), F32),
            pltpu.VMEM((DX, 8, 128), F32),
            pltpu.VMEM((DY, 8, 128), F32),
            pltpu.VMEM((2, 8, 128), F32),
            field,
            pltpu.VMEM((8, 128), F32),
            pltpu.VMEM((8, 128), F32),
            pltpu.SemaphoreType.DMA((8,)),
            pltpu.SemaphoreType.DMA((8,)),
            pltpu.SemaphoreType.DMA((DX,)),
            pltpu.SemaphoreType.DMA((DX,)),
            pltpu.SemaphoreType.DMA((DY,)),
            pltpu.SemaphoreType.DMA((DY,)),
        ],
        compiler_params=pltpu.CompilerParams(
            collective_id=0, has_side_effects=True, vmem_limit_bytes=40 * 1024 * 1024
        ),
    )(
        facies, source, facies_perm, facies_store,
        well_x.reshape(1, WELLS), well_y.reshape(1, WELLS), well_rate.reshape(1, WELLS),
    )


def solution(mesh):
    in_specs = (P("gx", "gy", None), P("gx", "gy", None), P(), P(), P(), P(), P())
    return jax.shard_map(
        per_device, mesh=mesh, in_specs=in_specs, out_specs=P("gx", "gy", None), check_vma=False
    )
```

time: 361 us -> 51.2 us (0.14)
  the two profiles are of different devices: /device:TPU:95 before, /device:TPU:1 now
where the time goes in v1:
time: 51.2 us; the launch traced here: 51 us
  Pallas kernels  48 us (94%)
  local copies, waits for them, and re-layouts  3.01 us (6%)
    pallas_call x1, Pallas kernels, per_device(): pl.pallas_call(kernel, out_shape=jax.ShapeDtypeStruct((TX, TY, CELLS_Z),...  48 us
    unnamed x15, local copies, waits for them, and re-layouts  3.01 us

profile of v1, /device:TPU:1, one launch (start us, length us, event | category | flops | bytes accessed | tf_op | source)
XLA Modules:
  0.0 51.0 jit_solution(270832068623601818)
XLA Ops:
  0.0 0.0 copy-start.5
  0.0 0.0 copy-start.6
  0.0 0.0 copy-start.2
  0.0 0.0 copy-start.3
  0.0 0.0 copy-start.4
  0.0 0.6 %copy-done.5 = s32[64]{0:T(128)S(1)} copy-done((s32[64]{0:T(128)S(1)}, s32[64]{0:T(128)}, u32[]{:S(2)}) %copy-start.5) | copy-done | bytes 280
  0.7 0.0 copy-done.6
  0.7 0.0 copy-done.2
  0.7 0.0 copy-done.3
  0.7 0.0 copy-done.4
  0.7 0.0 copy-start
  0.7 0.8 %copy-done = s32[8,16,128]{2,1,0:T(8,128)S(1)} copy-done((s32[8,16,128]{2,1,0:T(8,128)S(1)}, s32[8,16,128]{2,1,0:T(8,128)}, u32[]{:S(2)}) %copy-start) | copy-done | bytes 65560
  1.6 0.0 copy-start.1
  1.6 0.8 %copy-done.1 = f32[8,16,128]{2,1,0:T(8,128)S(1)} copy-done((f32[8,16,128]{2,1,0:T(8,128)S(1)}, f32[8,16,128]{2,1,0:T(8,128)}, u32[]{:S(2)}) %copy-start.1) | copy-done | bytes 65560
  2.4 48.0 %shard_map.73 = f32[8,16,128]{2,1,0:T(8,128)S(1)} custom-call(s32[8,16,128]{2,1,0:T(8,128)S(1)} %copy-done, f32[8,16,128]{2,1,0:T(8,128)S(1)} %copy-done.1, f32[8]{0:T(128)S(1)} %copy-done.2, f32[8]{0:T(128)S(1)} %copy-done.3, s32[1,64]{1,0:T(1,128)S(1)} %bitcast.3, s32[1,64]{1,0:T(1,128)S(1)} %bitcast.4, f32[1,64]{1,0:T(1,128)S(1)} %bitcast.5), custom_call_target="tpu_custom_call" | custom-call | tf_op jit(solution)/shard_map/pallas_call | solution.py:393
  50.4 0.6 %copy.9 = f32[8,16,128]{2,1,0:T(8,128)} copy(f32[8,16,128]{2,1,0:T(8,128)S(1)} %shard_map.73) | data formatting | bytes 131072
Async XLA Ops:
  0.0 0.7 %copy-start.5 = (s32[64]{0:T(128)S(1)}, s32[64]{0:T(128)}, u32[]{:S(2)}) copy-start(s32[64]{0:T(128)} %param.12) | copy-start | bytes 772
  0.0 0.7 %copy-start.6 = (f32[64]{0:T(128)S(1)}, f32[64]{0:T(128)}, u32[]{:S(2)}) copy-start(f32[64]{0:T(128)} %param.13) | copy-start | bytes 772
  0.0 0.7 %copy-start.2 = (f32[8]{0:T(128)S(1)}, f32[8]{0:T(128)}, u32[]{:S(2)}) copy-start(f32[8]{0:T(128)} %perm_ref.1) | copy-start | bytes 100
  0.0 0.7 %copy-start.3 = (f32[8]{0:T(128)S(1)}, f32[8]{0:T(128)}, u32[]{:S(2)}) copy-start(f32[8]{0:T(128)} %store_ref.1) | copy-start | bytes 100
  0.0 0.7 %copy-start.4 = (s32[64]{0:T(128)S(1)}, s32[64]{0:T(128)}, u32[]{:S(2)}) copy-start(s32[64]{0:T(128)} %param.11) | copy-start | bytes 772
  0.7 0.8 %copy-start = (s32[8,16,128]{2,1,0:T(8,128)S(1)}, s32[8,16,128]{2,1,0:T(8,128)}, u32[]{:S(2)}) copy-start(s32[8,16,128]{2,1,0:T(8,128)} %facies_ref.1) | copy-start | bytes 196612
  1.6 0.8 %copy-start.1 = (f32[8,16,128]{2,1,0:T(8,128)S(1)}, f32[8,16,128]{2,1,0:T(8,128)}, u32[]{:S(2)}) copy-start(f32[8,16,128]{2,1,0:T(8,128)} %source_ref.1) | copy-start | bytes 196612

commit v2 on v1

--- a/solution.py
+++ b/solution.py
@@ -20,9 +20,7 @@
 MESH = pl.DeviceIdType.MESH
 F32 = jnp.float32
 
-COLORS = [(c >> 2 & 1, c >> 1 & 1, c & 1) for c in range(8)]
-SLOT = [4 * i + j + 8 * k for i, j, k in COLORS]
-RHS_SLOT = 2
+COLORS = [(c >> 2 & 1, c & 1, c >> 1 & 1) for c in range(8)]
 
 
 def roll(value, shift):
@@ -50,22 +48,31 @@
 
 
 def kernel(
-    facies_ref, source_ref, perm_ref, store_ref, wx_ref, wy_ref, wr_ref, out_ref,
-    fac, hperm, stor, coef, trans, wdiag, va, vb, bv, rhs, wide, stage1, stage2, val, prol,
-    mine, half, hsend, hrecv, xsend, xrecv, ysend, yrecv,
+    facies_hbm, source_hbm, perm_ref, store_ref, wx_hbm, wy_hbm, wr_hbm, out_ref,
+    fac, hperm, stor, coef, trans, wdiag, va, vb, bv, rim, rimy, rhs, wide, stage1, stage2, val, prol,
+    mine, half, source_ref, wx_ref, wy_ref, wr_ref,
+    insem, hsend, hrecv, xsend, xrecv, ysend, yrecv,
 ):
     gx = lax.axis_index("gx")
     gy = lax.axis_index("gy")
     ax, ay = gx * TX, gy * TY
     lane, sub = iota(1), iota(0)
 
+    inputs = [
+        pltpu.make_async_copy(facies_hbm, fac.at[pl.ds(HX, TX), pl.ds(HY, TY)], insem.at[0]),
+        pltpu.make_async_copy(source_hbm, source_ref, insem.at[1]),
+        pltpu.make_async_copy(wx_hbm, wx_ref, insem.at[2]),
+        pltpu.make_async_copy(wy_hbm, wy_ref, insem.at[3]),
+        pltpu.make_async_copy(wr_hbm, wr_ref, insem.at[4]),
+    ]
     barrier = pltpu.get_barrier_semaphore()
-    partners = [((gx + d) % DX, gy) for d in range(1, DX)]
-    partners += [(gx, (gy + d) % DY) for d in range(1, DY)]
-    corners = [((gx + i) % DX, (gy + j) % DY) for i in (1, DX - 1) for j in (1, DY - 1)]
-    for who in partners + corners:
+    near = [((gx + i) % DX, (gy + j) % DY) for i in (0, 1, DX - 1) for j in (0, 1, DY - 1) if i or j]
+    far = [((gx + d) % DX, gy) for d in range(2, DX - 1)] + [(gx, (gy + d) % DY) for d in range(2, DY - 1)]
+    for who in near + far:
         pl.semaphore_signal(barrier, inc=1, device_id=who, device_id_type=MESH)
-    pl.semaphore_wait(barrier, len(partners) + 4)
+    for copy in inputs:
+        copy.start()
+    pl.semaphore_wait(barrier, len(near) + len(far))
 
     copies = []
     n = 0
@@ -79,7 +86,7 @@
             ty = {1: 0, -1: HY + TY, 0: HY}[dy]
             copies.append(
                 pltpu.make_async_remote_copy(
-                    src_ref=facies_ref.at[pl.ds(sx[0], sx[1]), pl.ds(sy[0], sy[1])],
+                    src_ref=facies_hbm.at[pl.ds(sx[0], sx[1]), pl.ds(sy[0], sy[1])],
                     dst_ref=fac.at[pl.ds(tx, sx[1]), pl.ds(ty, sy[1])],
                     send_sem=hsend.at[n],
                     recv_sem=hrecv.at[n],
@@ -91,6 +98,8 @@
     for copy in copies:
         copy.start()
 
+    for copy in inputs[1:]:
+        copy.wait()
     well_x = wx_ref[...]
     well_y = wy_ref[...]
     well_r = wr_ref[...]
@@ -114,9 +123,7 @@
 
     lax.fori_loop(0, EX, start_plane, 0)
 
-    fac[HX : HX + TX, HY : HY + TY, :] = facies_ref[...]
-    for copy in copies:
-        copy.wait()
+    inputs[0].wait()
 
     half_inv = [0.5 / jnp.full((8, 128), perm_ref[f], F32) for f in range(FACIES)]
     store_at = [jnp.full((8, 128), store_ref[f], F32) for f in range(FACIES)]
@@ -127,14 +134,22 @@
             table = [jnp.where(bits[b], hi, lo) for lo, hi in zip(table[::2], table[1::2])]
         return table[0]
 
-    def lookup_plane(x, _):
-        for t in range(4):
-            code = fac[x, 8 * t : 8 * t + 8, :]
-            hperm[x, 8 * t : 8 * t + 8, :] = pick(code, half_inv)
-            stor[x, 8 * t : 8 * t + 8, :] = pick(code, store_at)
-        return 0
-
-    lax.fori_loop(0, EX, lookup_plane, 0)
+    def lookup(tiles):
+        def plane(x, _):
+            for t in tiles:
+                code = fac[x, 8 * t : 8 * t + 8, :]
+                hperm[x, 8 * t : 8 * t + 8, :] = pick(code, half_inv)
+                stor[x, 8 * t : 8 * t + 8, :] = pick(code, store_at)
+            return 0
+
+        return plane
+
+    lax.fori_loop(HX, HX + TX, lookup((1, 2)), 0)
+    for copy in copies:
+        copy.wait_recv()
+    lax.fori_loop(0, HX, lookup(range(4)), 0)
+    lax.fori_loop(HX, HX + TX, lookup((0, 3)), 0)
+    lax.fori_loop(HX + TX, EX, lookup(range(4)), 0)
 
     last_z = flag(lane < CELLS_Z - 1)
 
@@ -216,25 +231,96 @@
                 q += k[3] * (v - yp[py] * basis[c, x, r + 1 : r + 9, :])
                 q += k[4] * (v - zm[pz] * roll(v, 1)) + k[5] * (v - zp[pz] * roll(v, -1))
                 bv[c, x - HX, 8 * t : 8 * t + 8, :] = q
+                rimy[c, x - HX, 8 * t : 8 * t + 8, :] = (
+                    (ym[1 - py] - 1.0) * k[2] * basis[c, x, r - 1 : r + 7, :]
+                    + (yp[1 - py] - 1.0) * k[3] * basis[c, x, r + 1 : r + 9, :]
+                )
         return 0
 
     lax.fori_loop(HX, HX + TX, apply_plane, 0)
+
+    west = lane < 64
+    cut_lo = [1.0 - same_z(lane, p) for p in range(2)]
+    cut_hi = [1.0 - same_z(lane - 1, p) for p in range(2)]
+    turn = lane % 32 >= 16
+
+    def rim_plane(x, acc):
+        acc = list(acc)
+        for t in range(2):
+            r = HY + 8 * t
+            tzm, tzp = trans[4, x, r : r + 8, :], trans[5, x, r : r + 8, :]
+            lo = [-tzp * cut_lo[1 - p] for p in range(2)]
+            hi = [-tzm * cut_hi[1 - p] for p in range(2)]
+            both = -tzp * (cut_lo[0] + cut_lo[1])
+            vs = [basis[c, x, r : r + 8, :] for c in range(8)]
+            up = [roll(v, -1) for v in vs]
+            for c, (px, py, pz) in enumerate(COLORS):
+                rim[c, x - HX, 8 * t : 8 * t + 8, :] = lo[pz] * up[c] + hi[pz] * roll(vs[c], 1)
+            here = [jnp.where(turn, vs[c], vs[c + 2]) for c in (0, 1, 4, 5)]
+            there = [jnp.where(turn, up[c], up[c + 2]) for c in (0, 1, 4, 5)]
+            first = [both * jnp.where(west, a, b) for a, b in zip(here, there)]
+            second = [jnp.where(west, b, a) for a, b in zip(here, there)]
+            for m in range(4):
+                for n in range(4):
+                    acc[4 * m + n] = acc[4 * m + n] + first[m] * second[n]
+        return tuple(acc)
+
+    zeros16 = tuple(jnp.zeros((8, 128), F32) for _ in range(16))
+    acc = lax.fori_loop(HX, HX + TX, rim_plane, zeros16)
+    for n in range(8, 16):
+        wide[n] = jnp.zeros((8, 128), F32)
+    corner4 = (0, 1, 4, 5)
+    for m in range(4):
+        for n in range(4):
+            wide[8 + m, corner4[n] : corner4[n] + 1, :] = jnp.sum(acc[4 * m + n], axis=0, keepdims=True)
+
+    parity_y = jnp.where(gy == 9, 1, 0)
+    at_rim = jnp.where((gy == 5) | (gy == 9), -1.0, 0.0).astype(F32)
+    top = flag(sub == 7) * at_rim
+
+    def rim_y_plane(x, acc):
+        acc = list(acc)
+        t = trans[3, x, HY + 8 : HY + 16, :] * top
+        here = [t * basis[c + parity_y, x, HY + 8 : HY + 16, :] for c in (0, 2, 4, 6)]
+        there = [basis[c + parity_y, x, HY + 9 : HY + 17, :] for c in (0, 2, 4, 6)]
+        for m in range(4):
+            for n in range(4):
+                acc[4 * m + n] = acc[4 * m + n] + here[m] * there[n]
+        return tuple(acc)
+
+    acc = lax.fori_loop(HX, HX + TX, rim_y_plane, zeros16)
+    for m in range(4):
+        for n in range(4):
+            line = jnp.sum(acc[4 * m + n], axis=0, keepdims=True)
+            wide[12 + m, 2 * n : 2 * n + 1, :] = line
+            wide[12 + n, 2 * m + 1 : 2 * m + 2, :] = line
 
     pairs = [(a, c) for a in range(8) for c in range(a, 8)]
     for group in (pairs[:15], pairs[15:30], pairs[30:]):
         rows = sorted({a for a, _ in group})
         cols = sorted({c for _, c in group})
-        last = group is not None and group[-1] == (7, 7)
+        last = group[-1] == (7, 7)
 
         def gather(x, acc, group=group, rows=rows, cols=cols, last=last):
             acc = list(acc)
             for t in range(2):
-                left = {a: basis[a, x + HX, HY + 8 * t : HY + 8 * t + 8, :] for a in (range(8) if last else rows)}
-                right = {c: bv[c, x, 8 * t : 8 * t + 8, :] for c in cols}
+                r = HY + 8 * t
+                at = slice(8 * t, 8 * t + 8)
+                left = {a: basis[a, x + HX, r : r + 8, :] for a in (range(8) if last else rows)}
+                right = {c: bv[c, x, at, :] for c in cols}
+                own = {c: basis[c, x + HX, r : r + 8, :] for c in cols}
+                over_z = {a: rim[a, x, at, :] for a in rows}
+                over_y = {a: rimy[a, x, at, :] for a in rows}
                 for n, (a, c) in enumerate(group):
                     acc[n] = acc[n] + left[a] * right[c]
+                    if COLORS[a][2] != COLORS[c][2] and COLORS[a][1] != COLORS[c][1]:
+                        acc[n] = acc[n] + own[c] * (over_z[a] + over_y[a])
+                    elif COLORS[a][2] != COLORS[c][2]:
+                        acc[n] = acc[n] + own[c] * over_z[a]
+                    elif COLORS[a][1] != COLORS[c][1]:
+                        acc[n] = acc[n] + own[c] * over_y[a]
                 if last:
-                    load = rhs[x, 8 * t : 8 * t + 8, :]
+                    load = rhs[x, at, :]
                     for a in range(8):
                         acc[len(group) + a] = acc[len(group) + a] + left[a] * load
             return tuple(acc)
@@ -248,15 +334,20 @@
                 wide[a, c : c + 1, :] = line
         if last:
             for a in range(8):
-                wide[8, a : a + 1, :] = jnp.sum(acc[len(group) + a], axis=0, keepdims=True)
-
-    packed = jnp.zeros((8, 128), F32)
-    for n in range(9):
-        line = wide[n]
-        for step in (1, 2, 4, 8):
-            line = line + roll(line, -step)
-        line = jnp.where(lane % 16 == 8, line, 0.0)
-        packed = packed + roll(line, 8 + (SLOT[n] if n < 8 else RHS_SLOT))
+                wide[16, a : a + 1, :] = jnp.sum(acc[len(group) + a], axis=0, keepdims=True)
+
+    def ranges(places):
+        total = jnp.zeros((8, 128), F32)
+        for n, slot in places:
+            line = wide[n]
+            for step in (1, 2, 4, 8):
+                line = line + roll(line, -step)
+            line = jnp.where(lane % 16 == 8, line, 0.0)
+            total = total + roll(line, 8 + slot)
+        return total
+
+    mine[0:8, :] = ranges([(n, n) for n in range(8)] + [(8 + m, 8 + corner4[m]) for m in range(4)])
+    mine[8:16, :] = ranges([(12 + m, 2 * m) for m in range(4)] + [(16, 1)])
 
     def exchange(src, slots, send, recv, axis):
         me = gx if axis == 0 else gy
@@ -272,84 +363,183 @@
             sent.append(copy)
         slots[me] = src[...]
         for copy in sent:
-            copy.wait()
+            copy.wait_recv()
+        return sent
 
     def tree(items):
         while len(items) > 1:
             items = [a + b for a, b in zip(items[::2], items[1::2])] + (items[-1:] if len(items) % 2 else [])
         return items[0]
 
-    mine[...] = packed
-    exchange(mine, stage1, xsend, xrecv, 0)
+    sent = exchange(mine, stage1, xsend, xrecv, 0)
     half[...] = tree([stage1[n] for n in range(DX)])
-    exchange(half, stage2, ysend, yrecv, 1)
-    sa = tree([stage2[n] for n in range(0, 6)])
-    sb = tree([stage2[n] for n in range(6, 10)])
-    sc = tree([stage2[n] for n in range(10, 16)])
-
-    pair_j = lane % 4
-    low = pair_j < 2
+    sent += exchange(half, stage2, ysend, yrecv, 1)
+
+    def parts(rows):
+        return [tree([stage2[n, rows : rows + 8, :] for n in range(*ends)]) for ends in ((0, 6), (6, 10), (10, 16))]
+
+    pa, pb, pc = parts(0)
+    qa, qb, qc = parts(8)
+    slot = lane % 16
+    ly, sy = lane % 2, sub % 2
+    lk, sk = lane // 2 % 2, sub // 2 % 2
+
+    def keep(cond, value):
+        return jnp.where(cond, value, 0.0)
+
+    def rows_up(value, shift):
+        return pltpu.roll(value, shift % 8, 0)
+
+    m00, m01 = (ly == 0) & (sy == 0), (ly == 0) & (sy == 1)
+    m10, m11 = (ly == 1) & (sy == 0), (ly == 1) & (sy == 1)
+    pairs_y = (slot < 8) & (lk < 2)
+    y01 = keep(pairs_y & m00, qa) + keep(pairs_y & m11, rows_up(roll(qb, 1), 1))
+    y10 = keep(pairs_y & m00, rows_up(qa, -1)) + keep(pairs_y & m11, roll(qb, 1))
+    joined = [[pa + keep(m11, pb), keep(m10, pb) + y01], [keep(m01, pb) + y10, pc + keep(m00, pb)]]
+    by_row = []
+    for pk in range(2):
+        picked = [[keep(lk == pk, joined[h][g]) for g in range(2)] for h in range(2)]
+        by_row.append([
+            (picked[0][g] + roll(picked[1][g], 2)) if pk == 0 else (roll(picked[0][g], -2) + picked[1][g])
+            for g in range(2)
+        ])
+
+    def by_column(values, pk):
+        low, high = keep(sk == pk, values[0]), keep(sk == pk, values[1])
+        return low + rows_up(high, 2) if pk == 0 else rows_up(low, -2) + high
+
+    node = [[by_column(by_row[pk], pq) for pq in range(2)] for pk in range(2)]
+    loads = [qa + keep(sy == 1, qb), qc + keep(sy == 0, qb)]
+    load_of = [by_column(loads, pk) for pk in range(2)]
+    layer = lane // 16
+    even = layer % 2 == 0
+    own = jnp.where(even, node[0][0] + roll(node[0][0], -16), node[1][1] + roll(node[1][1], -16))
+    near_k = jnp.where(even, node[0][1], node[1][0])
+    near_up = jnp.where(even, roll(node[0][1], -16), roll(node[1][0], -16))
+    near_k = jnp.where(layer < 4, near_up, near_k)
+    far_k = jnp.where(layer < 4, roll(node[0][0], -24), roll(node[0][0], 8))
+    load_k = jnp.where(even, load_of[0] + roll(load_of[0], -16), load_of[1] + roll(load_of[1], -16))
+
+    def ends(value, level, at):
+        a, b = 16 * level + at, 16 * (7 - level) + at
+        return jnp.where(west, jnp.broadcast_to(value[:, a : a + 1], (8, 128)), jnp.broadcast_to(value[:, b : b + 1], (8, 128)))
+
+    def all_lanes(value, at):
+        return jnp.broadcast_to(value[:, at : at + 1], (8, 128))
+
+    def spread(value, k):
+        return jnp.broadcast_to(value[k : k + 1, :], (8, 128))
+
+    def eliminate(block, nexts, load, after):
+        block, nexts = list(block), [list(b) for b in nexts]
+        load = [spread(load, k) for k in range(8)]
+        for k in range(8):
+            inverse = 1.0 / spread(block[k], k)
+            pivot = block[k] * inverse
+            scaled = [b[k] * inverse for b in nexts]
+            scaled_load = load[k] * inverse
+            after([b[k] for b in nexts], scaled, scaled_load)
+            for i in range(8):
+                if i == k:
+                    continue
+                f = spread(block[i], k)
+                block[i] = block[i] - f * pivot
+                for b, v in zip(nexts, scaled):
+                    b[i] = b[i] - f * v
+                load[i] = load[i] - f * scaled_load
+            block[k] = pivot
+            for b, v in zip(nexts, scaled):
+                b[k] = v
+            load[k] = scaled_load
+        return nexts, load
+
+    diag = [[ends(own, l, i) for i in range(8)] for l in range(3)]
+    one = [[ends(near_k, l, i) for i in range(8)] for l in range(3)]
+    two = [[ends(far_k, l, i) for i in range(8)] for l in range(3)]
+    right = [ends(load_k, l, 1) for l in range(3)]
     zero = jnp.zeros((8, 128), F32)
-
-    def put(j0=zero, j1=zero, j2=zero, j3=zero):
-        first = jnp.where(pair_j == 0, j0, jnp.where(pair_j == 1, j1, 0.0))
-        second = jnp.where(pair_j == 0, j2, jnp.where(pair_j == 1, j3, 0.0))
-        return first + roll(second, 2)
-
-    line_of = [
-        put(sa, sa),
-        put(sa, sa + sb, sb),
-        put(zero, sb, sb + sc, sc),
-        put(zero, zero, sc, sc),
-    ]
-    load_of = [sa, sa + sb, sb + sc, sc]
-    group = lane // 16
-    used = lane % 16 < 8
-    even = sub % 2 == 0
-    on = used & (group == sub)
-    above = used & (group == sub + 1)
-    below = used & (group == sub - 1)
-    matrix = []
-    for ij in range(8):
-        i, j = ij // 4, ij % 4
-        e = 4 * i + 2 * (j % 2)
-        base = line_of[j]
-        turns = {s: roll(base, -s) for s in (8, 16, 24)}
-        turns[0] = base
-        be = {s: jnp.broadcast_to(v[e : e + 1, :], (8, 128)) for s, v in turns.items()}
-        bo = {s: jnp.broadcast_to(v[e + 1 : e + 2, :], (8, 128)) for s, v in turns.items()}
-        diag_part = jnp.where(even, be[0] + be[16], bo[8] + bo[24])
-        up = jnp.where(even, be[8], bo[0])
-        down = jnp.where(even, be[24], bo[16])
-        block = jnp.where(on, diag_part, jnp.where(above, up, jnp.where(below, down, 0.0)))
-        load = jnp.where(lane % 16 == RHS_SLOT, load_of[j], 0.0)
-        load = load + roll(load, -16)
-        le = jnp.broadcast_to(load[e : e + 1, :], (8, 128))
-        lo = jnp.broadcast_to(load[e + 1 : e + 2, :], (8, 128))
-        load = jnp.where((group == sub) & (lane % 16 == RHS_SLOT), jnp.where(even, le, lo), 0.0)
-        load = jnp.sum(load, axis=1, keepdims=True)
-        matrix.append(jnp.where(lane == 8, load, block))
-
-    for kk in range(8):
-        for ij in range(8):
-            at = 16 * kk + ij
-            columns = [m[:, at : at + 1] for m in matrix]
-            row = jnp.broadcast_to(matrix[ij][kk : kk + 1, :], (8, 128))
-            pivot = jnp.broadcast_to(columns[ij][kk : kk + 1, :], (8, 1))
-            row = row / pivot
-            for n in range(8):
-                update = matrix[n] - columns[n] * row
-                if n == ij:
-                    update = jnp.where(sub == kk, row, update)
-                matrix[n] = update
+    d3, d4, d34 = [zero] * 8, [zero] * 8, [zero] * 8
+    r3, r4 = zero, zero
+    solved = []
+    for level in range(3):
+        def after(raw, scaled, load, level=level):
+            nonlocal r3, r4
+            p1, p2 = raw
+            s1, s2 = scaled
+            for i in range(8):
+                f1, f2 = spread(p1, i), spread(p2, i)
+                if level == 0:
+                    diag[1][i] = diag[1][i] - f1 * s1
+                    one[1][i] = one[1][i] - f1 * s2
+                    diag[2][i] = diag[2][i] - f2 * s2
+                elif level == 1:
+                    diag[2][i] = diag[2][i] - f1 * s1
+                    one[2][i] = one[2][i] - f1 * s2
+                    d3[i] = d3[i] - f2 * s2
+                else:
+                    d3[i] = d3[i] - f1 * s1
+                    d4[i] = d4[i] - f2 * s2
+                    d34[i] = d34[i] - jnp.where(west, f1, f2) * jnp.where(west, s2, s1)
+            if level == 0:
+                right[1] = right[1] - p1 * load
+                right[2] = right[2] - p2 * load
+            elif level == 1:
+                right[2] = right[2] - p1 * load
+                r3 = r3 - p2 * load
+            else:
+                r3 = r3 - p1 * load
+                r4 = r4 - p2 * load
+
+        solved.append(eliminate(diag[level], [one[level], two[level]], right[level], after))
+
+    def meet(a, b):
+        value = jnp.where(west, a, b)
+        return value + roll(value, 64)
+
+    m3 = [all_lanes(own, 48 + i) + meet(d3[i], d4[i]) for i in range(8)]
+    m4 = [all_lanes(own, 64 + i) + meet(d4[i], d3[i]) for i in range(8)]
+    m34 = [all_lanes(near_k, 48 + i) + d34[i] + roll(d34[i], 64) for i in range(8)]
+    v3 = all_lanes(load_k, 49) + meet(r3, r4)
+    v4 = all_lanes(load_k, 65) + meet(r4, r3)
+
+    def after_three(raw, scaled, load):
+        nonlocal v4
+        for i in range(8):
+            m4[i] = m4[i] - spread(raw[0], i) * scaled[0]
+        v4 = v4 - raw[0] * load
+
+    (up3,), load3 = eliminate(m3, [m34], v3, after_three)
+    _, x4 = eliminate(m4, [], v4, lambda *_: None)
+
+    def column(items):
+        value = items[0]
+        for i in range(1, 8):
+            value = jnp.where(sub == i, items[i], value)
+        return value
+
+    def total(value):
+        return jnp.broadcast_to(jnp.sum(value, axis=0, keepdims=True), (8, 128))
+
+    c4 = column(x4)
+    x3 = [load3[i] - total(up3[i] * c4) for i in range(8)]
+    c3 = column(x3)
+    first, second = jnp.where(west, c3, c4), jnp.where(west, c4, c3)
+    x_of = [None] * 3
+    for level in (2, 1, 0):
+        (n1, n2), load = solved[level]
+        x_of[level] = [load[i] - total(n1[i] * first + n2[i] * second) for i in range(8)]
+        first, second = column(x_of[level]), first
 
     node_k = [2 * ((lane + BLOCK_Z // 2) // (2 * BLOCK_Z)),
               2 * ((lane + BLOCK_Z // 2 + BLOCK_Z) // (2 * BLOCK_Z)) - 1]
-    for ij in range(8):
-        u = matrix[ij][:, 8:9]
-        for p in range(2):
-            line = jnp.sum(jnp.where(node_k[p] == sub, u, 0.0), axis=0, keepdims=True)
-            val[p, ij : ij + 1, :] = line
+    for p in range(2):
+        k = node_k[p]
+        at = [((k == level) & west) | ((k == 7 - level) & ~west) for level in range(3)]
+        for ij in range(8):
+            line = keep(k == 3, x3[ij]) + keep(k == 4, x4[ij])
+            for level in range(3):
+                line = jnp.where(at[level], x_of[level][ij], line)
+            val[p, ij : ij + 1, :] = line[0:1, :]
 
     def node_row(px, py, pz, tile):
         first = tile * TY
@@ -368,6 +558,9 @@
             return 0
 
         lax.fori_loop(HX - 1, HX + TX + 1, prolong, 0)
+
+    for copy in copies + sent:
+        copy.wait_send()
 
     def finish(x, _):
         for t in range(2):
@@ -388,12 +581,13 @@
 def per_device(facies, source, facies_perm, facies_store, well_x, well_y, well_rate):
     vmem = pl.BlockSpec(memory_space=pltpu.VMEM)
     smem = pl.BlockSpec(memory_space=pltpu.SMEM)
+    hbm = pl.BlockSpec(memory_space=pltpu.HBM)
     field = pltpu.VMEM((EX, EY, 128), F32)
     colors = pltpu.VMEM((8, EX, EY, 128), F32)
     return pl.pallas_call(
         kernel,
         out_shape=jax.ShapeDtypeStruct((TX, TY, CELLS_Z), F32),
-        in_specs=[vmem, vmem, smem, smem, vmem, vmem, vmem],
+        in_specs=[hbm, hbm, smem, smem, hbm, hbm, hbm],
         out_specs=vmem,
         scratch_shapes=[
             pltpu.VMEM((EX, EY, 128), jnp.int32),
@@ -405,14 +599,21 @@
             colors,
             colors,
             pltpu.VMEM((8, TX, TY, 128), F32),
+            pltpu.VMEM((8, TX, TY, 128), F32),
+            pltpu.VMEM((8, TX, TY, 128), F32),
             pltpu.VMEM((TX, TY, 128), F32),
-            pltpu.VMEM((9, 8, 128), F32),
-            pltpu.VMEM((DX, 8, 128), F32),
-            pltpu.VMEM((DY, 8, 128), F32),
+            pltpu.VMEM((17, 8, 128), F32),
+            pltpu.VMEM((DX, 16, 128), F32),
+            pltpu.VMEM((DY, 16, 128), F32),
             pltpu.VMEM((2, 8, 128), F32),
             field,
-            pltpu.VMEM((8, 128), F32),
-            pltpu.VMEM((8, 128), F32),
+            pltpu.VMEM((16, 128), F32),
+            pltpu.VMEM((16, 128), F32),
+            pltpu.VMEM((TX, TY, 128), F32),
+            pltpu.VMEM((1, WELLS), jnp.int32),
+            pltpu.VMEM((1, WELLS), jnp.int32),
+            pltpu.VMEM((1, WELLS), F32),
+            pltpu.SemaphoreType.DMA((5,)),
             pltpu.SemaphoreType.DMA((8,)),
             pltpu.SemaphoreType.DMA((8,)),
             pltpu.SemaphoreType.DMA((DX,)),

time: 51.2 us -> 46.1 us (0.900)
  Pallas kernels: 48 us -> 42.9 us
    pallas_call x1, Pallas kernels: 48 us -> 42.9 us  [per_device(): pl.pallas_call(kernel, out_shape=jax.ShapeDtypeStruct((TX, TY, CELLS_Z),...]
where the time goes in v2:
time: 46.1 us; the launch traced here: 45.9 us
  Pallas kernels  42.9 us (93%)
  local copies, waits for them, and re-layouts  3.01 us (7%)
    pallas_call x1, Pallas kernels, per_device(): pl.pallas_call(kernel, out_shape=jax.ShapeDtypeStruct((TX, TY, CELLS_Z),...  42.9 us
    unnamed x15, local copies, waits for them, and re-layouts  3.01 us

profile of v2, /device:TPU:1, one launch (start us, length us, event | category | flops | bytes accessed | tf_op | source)
XLA Modules:
  0.0 45.9 jit_solution(9690848501954113182)
XLA Ops:
  0.0 0.0 copy-start.5
  0.0 0.0 copy-start.6
  0.0 0.0 copy-start.2
  0.0 0.0 copy-start.3
  0.0 0.0 copy-start.4
  0.0 0.6 %copy-done.5 = s32[64]{0:T(128)S(1)} copy-done((s32[64]{0:T(128)S(1)}, s32[64]{0:T(128)}, u32[]{:S(2)}) %copy-start.5) | copy-done | bytes 280
  0.7 0.0 copy-done.6
  0.7 0.0 copy-done.2
  0.7 0.0 copy-done.3
  0.7 0.0 copy-done.4
  0.7 0.0 copy-start
  0.7 0.8 %copy-done = s32[8,16,128]{2,1,0:T(8,128)S(1)} copy-done((s32[8,16,128]{2,1,0:T(8,128)S(1)}, s32[8,16,128]{2,1,0:T(8,128)}, u32[]{:S(2)}) %copy-start) | copy-done | bytes 65560
  1.6 0.0 copy-start.1
  1.6 0.8 %copy-done.1 = f32[8,16,128]{2,1,0:T(8,128)S(1)} copy-done((f32[8,16,128]{2,1,0:T(8,128)S(1)}, f32[8,16,128]{2,1,0:T(8,128)}, u32[]{:S(2)}) %copy-start.1) | copy-done | bytes 65560
  2.4 42.9 %shard_map.73 = f32[8,16,128]{2,1,0:T(8,128)S(1)} custom-call(s32[8,16,128]{2,1,0:T(8,128)S(1)} %copy-done, f32[8,16,128]{2,1,0:T(8,128)S(1)} %copy-done.1, f32[8]{0:T(128)S(1)} %copy-done.2, f32[8]{0:T(128)S(1)} %copy-done.3, s32[1,64]{1,0:T(1,128)S(1)} %bitcast.3, s32[1,64]{1,0:T(1,128)S(1)} %bitcast.4, f32[1,64]{1,0:T(1,128)S(1)} %bitcast.5), custom_call_target="tpu_custom_call" | custom-call | tf_op jit(solution)/shard_map/pallas_call | solution.py:587
  45.3 0.6 %copy.9 = f32[8,16,128]{2,1,0:T(8,128)} copy(f32[8,16,128]{2,1,0:T(8,128)S(1)} %shard_map.73) | data formatting | bytes 131072
Async XLA Ops:
  0.0 0.7 %copy-start.5 = (s32[64]{0:T(128)S(1)}, s32[64]{0:T(128)}, u32[]{:S(2)}) copy-start(s32[64]{0:T(128)} %param.12) | copy-start | bytes 772
  0.0 0.7 %copy-start.6 = (f32[64]{0:T(128)S(1)}, f32[64]{0:T(128)}, u32[]{:S(2)}) copy-start(f32[64]{0:T(128)} %param.13) | copy-start | bytes 772
  0.0 0.7 %copy-start.2 = (f32[8]{0:T(128)S(1)}, f32[8]{0:T(128)}, u32[]{:S(2)}) copy-start(f32[8]{0:T(128)} %perm_ref.1) | copy-start | bytes 100
  0.0 0.7 %copy-start.3 = (f32[8]{0:T(128)S(1)}, f32[8]{0:T(128)}, u32[]{:S(2)}) copy-start(f32[8]{0:T(128)} %store_ref.1) | copy-start | bytes 100
  0.0 0.7 %copy-start.4 = (s32[64]{0:T(128)S(1)}, s32[64]{0:T(128)}, u32[]{:S(2)}) copy-start(s32[64]{0:T(128)} %param.11) | copy-start | bytes 772
  0.7 0.8 %copy-start = (s32[8,16,128]{2,1,0:T(8,128)S(1)}, s32[8,16,128]{2,1,0:T(8,128)}, u32[]{:S(2)}) copy-start(s32[8,16,128]{2,1,0:T(8,128)} %facies_hbm.1) | copy-start | bytes 196612
  1.6 0.8 %copy-start.1 = (f32[8,16,128]{2,1,0:T(8,128)S(1)}, f32[8,16,128]{2,1,0:T(8,128)}, u32[]{:S(2)}) copy-start(f32[8,16,128]{2,1,0:T(8,128)} %source_hbm.1) | copy-start | bytes 196612

commit v3 on v2

--- a/solution.py
+++ b/solution.py
@@ -18,6 +18,7 @@
 EX, EY = TX + 2 * HX, TY + 2 * HY
 DX, DY = 16, 16
 MESH = pl.DeviceIdType.MESH
+UNROLL_SWEEP, UNROLL_COEF = True, 2
 F32 = jnp.float32
 
 COLORS = [(c >> 2 & 1, c & 1, c >> 1 & 1) for c in range(8)]
@@ -51,7 +52,7 @@
     facies_hbm, source_hbm, perm_ref, store_ref, wx_hbm, wy_hbm, wr_hbm, out_ref,
     fac, hperm, stor, coef, trans, wdiag, va, vb, bv, rim, rimy, rhs, wide, stage1, stage2, val, prol,
     mine, half, source_ref, wx_ref, wy_ref, wr_ref,
-    insem, hsend, hrecv, xsend, xrecv, ysend, yrecv,
+    insem, hsend, hrecv, xsend, xrecv, ysend, yrecv, news_x, news_y,
 ):
     gx = lax.axis_index("gx")
     gy = lax.axis_index("gy")
@@ -67,12 +68,22 @@
     ]
     barrier = pltpu.get_barrier_semaphore()
     near = [((gx + i) % DX, (gy + j) % DY) for i in (0, 1, DX - 1) for j in (0, 1, DY - 1) if i or j]
-    far = [((gx + d) % DX, gy) for d in range(2, DX - 1)] + [(gx, (gy + d) % DY) for d in range(2, DY - 1)]
-    for who in near + far:
+    for who in near:
         pl.semaphore_signal(barrier, inc=1, device_id=who, device_id_type=MESH)
     for copy in inputs:
         copy.start()
-    pl.semaphore_wait(barrier, len(near) + len(far))
+    pl.semaphore_wait(barrier, len(near))
+
+    def tell(n):
+        d = 1 << n
+        for i in (d, DX - d):
+            pl.semaphore_signal(news_x.at[n], inc=1, device_id=((gx + i) % DX, gy), device_id_type=MESH)
+        for j in (d, DY - d):
+            pl.semaphore_signal(news_y.at[n], inc=1, device_id=(gx, (gy + j) % DY), device_id_type=MESH)
+
+    def hear(n):
+        pl.semaphore_wait(news_x.at[n], 2)
+        pl.semaphore_wait(news_y.at[n], 2)
 
     copies = []
     n = 0
@@ -80,10 +91,11 @@
         for dy in (-1, 0, 1):
             if dx == 0 and dy == 0:
                 continue
-            sx = {1: (TX - HX, HX), -1: (0, HX), 0: (0, TX)}[dx]
-            sy = {1: (TY - HY, HY), -1: (0, HY), 0: (0, TY)}[dy]
-            tx = {1: 0, -1: HX + TX, 0: HX}[dx]
-            ty = {1: 0, -1: HY + TY, 0: HY}[dy]
+            wx = HX if dy == 0 else HX - 1
+            sx = {1: (TX - wx, wx), -1: (0, wx), 0: (0, TX)}[dx]
+            sy = {1: (TY - 4, 4), -1: (0, 4), 0: (0, TY)}[dy]
+            tx = {1: HX - wx, -1: HX + TX, 0: HX}[dx]
+            ty = {1: HY - 4, -1: HY + TY, 0: HY}[dy]
             copies.append(
                 pltpu.make_async_remote_copy(
                     src_ref=facies_hbm.at[pl.ds(sx[0], sx[1]), pl.ds(sy[0], sy[1])],
@@ -97,6 +109,7 @@
             n += 1
     for copy in copies:
         copy.start()
+    tell(0)
 
     for copy in inputs[1:]:
         copy.wait()
@@ -111,6 +124,15 @@
             column = jnp.sum(part, axis=1, keepdims=True)
             rhs[x, 8 * j : 8 * j + 8, :] = source_ref[x, 8 * j : 8 * j + 8, :] + column / CELLS_Z
 
+    last_z = flag(lane < CELLS_Z - 1)
+    row_at = [ay - HY + 4 + 8 * t + sub for t in range(3)]
+    row_m = [flag(inside(row - 1, GRID_Y) & inside(row, GRID_Y)) for row in row_at]
+    row_p = [flag(inside(row, GRID_Y) & inside(row + 1, GRID_Y)) for row in row_at]
+    same_ym = [[same_xy(row - 1, p, BLOCK_Y) for p in range(2)] for row in row_at]
+    same_yp = [[same_xy(row, p, BLOCK_Y) for p in range(2)] for row in row_at]
+    same_zm = [same_z(lane - 1, p) for p in range(2)]
+    same_zp = [same_z(lane, p) for p in range(2)]
+
     def start_plane(x, _):
         gxe = ax - HX + x
         for t in range(4):
@@ -151,7 +173,8 @@
     lax.fori_loop(HX, HX + TX, lookup((0, 3)), 0)
     lax.fori_loop(HX + TX, EX, lookup(range(4)), 0)
 
-    last_z = flag(lane < CELLS_Z - 1)
+    hear(0)
+    tell(1)
 
     def coef_plane(x, _):
         gxe = ax - HX + x
@@ -160,13 +183,10 @@
         for t in range(3):
             r = 4 + 8 * t
             h = hperm[x, r : r + 8, :]
-            row = ay - HY + r + sub
-            row_m = flag(inside(row - 1, GRID_Y) & inside(row, GRID_Y))
-            row_p = flag(inside(row, GRID_Y) & inside(row + 1, GRID_Y))
             txm = ok_m / (h + hperm[x - 1, r : r + 8, :])
             txp = ok_p / (h + hperm[x + 1, r : r + 8, :])
-            tym = row_m / (h + hperm[x, r - 1 : r + 7, :])
-            typ = row_p / (h + hperm[x, r + 1 : r + 9, :])
+            tym = row_m[t] / (h + hperm[x, r - 1 : r + 7, :])
+            typ = row_p[t] / (h + hperm[x, r + 1 : r + 9, :])
             tzp = last_z / (h + roll(h, -1))
             tzm = roll(tzp, 1)
             diag = stor[x, r : r + 8, :] + txm + txp + tym + typ + tzm + tzp
@@ -179,13 +199,13 @@
             for p in range(2):
                 coef[p, x, a : a + 8, :] = wxm * same_xy(gxe - 1, p, BLOCK_X)
                 coef[2 + p, x, a : a + 8, :] = wxp * same_xy(gxe, p, BLOCK_X)
-                coef[4 + p, x, a : a + 8, :] = wym * same_xy(row - 1, p, BLOCK_Y)
-                coef[6 + p, x, a : a + 8, :] = wyp * same_xy(row, p, BLOCK_Y)
-                coef[8 + p, x, a : a + 8, :] = wzm * same_z(lane - 1, p)
-                coef[10 + p, x, a : a + 8, :] = wzp * same_z(lane, p)
+                coef[4 + p, x, a : a + 8, :] = wym * same_ym[t][p]
+                coef[6 + p, x, a : a + 8, :] = wyp * same_yp[t][p]
+                coef[8 + p, x, a : a + 8, :] = wzm * same_zm[p]
+                coef[10 + p, x, a : a + 8, :] = wzp * same_zp[p]
         return 0
 
-    lax.fori_loop(1, EX - 1, coef_plane, 0)
+    lax.fori_loop(1, EX - 1, coef_plane, 0, unroll=UNROLL_COEF)
 
     def sweep(src, dst, low):
         def plane(x, _):
@@ -206,23 +226,25 @@
                     dst[c, x, r : r + 8, :] = new[c] + old[c] * keep
             return 0
 
-        lax.fori_loop(low, EX - low, plane, 0)
+        lax.fori_loop(low, EX - low, plane, 0, unroll=UNROLL_SWEEP)
 
     sweep(va, vb, 1)
+    hear(1)
+    tell(2)
     sweep(vb, va, 2)
     sweep(va, vb, 3)
     basis = vb
 
+    tile_rows = [ay + 8 * t + sub for t in range(2)]
+    tile_ym = [[same_xy(row - 1, p, BLOCK_Y) for p in range(2)] for row in tile_rows]
+    tile_yp = [[same_xy(row, p, BLOCK_Y) for p in range(2)] for row in tile_rows]
+
     def apply_plane(x, _):
         for t in range(2):
             r = HY + 8 * t
-            row = ay + 8 * t + sub
             k = [trans[n, x, r : r + 8, :] for n in range(6)]
             s = stor[x, r : r + 8, :]
-            ym = [same_xy(row - 1, p, BLOCK_Y) for p in range(2)]
-            yp = [same_xy(row, p, BLOCK_Y) for p in range(2)]
-            zm = [same_z(lane - 1, p) for p in range(2)]
-            zp = [same_z(lane, p) for p in range(2)]
+            ym, yp, zm, zp = tile_ym[t], tile_yp[t], same_zm, same_zp
             for c, (px, py, pz) in enumerate(COLORS):
                 v = basis[c, x, r : r + 8, :]
                 q = s * v
@@ -237,7 +259,7 @@
                 )
         return 0
 
-    lax.fori_loop(HX, HX + TX, apply_plane, 0)
+    lax.fori_loop(HX, HX + TX, apply_plane, 0, unroll=2)
 
     west = lane < 64
     cut_lo = [1.0 - same_z(lane, p) for p in range(2)]
@@ -266,10 +288,10 @@
         return tuple(acc)
 
     zeros16 = tuple(jnp.zeros((8, 128), F32) for _ in range(16))
-    acc = lax.fori_loop(HX, HX + TX, rim_plane, zeros16)
-    for n in range(8, 16):
+    acc = lax.fori_loop(HX, HX + TX, rim_plane, zeros16, unroll=2)
+    for n in range(8, 12):
         wide[n] = jnp.zeros((8, 128), F32)
-    corner4 = (0, 1, 4, 5)
+    corner4, edge4 = (0, 1, 4, 5), (2, 3, 6, 7)
     for m in range(4):
         for n in range(4):
             wide[8 + m, corner4[n] : corner4[n] + 1, :] = jnp.sum(acc[4 * m + n], axis=0, keepdims=True)
@@ -288,7 +310,7 @@
                 acc[4 * m + n] = acc[4 * m + n] + here[m] * there[n]
         return tuple(acc)
 
-    acc = lax.fori_loop(HX, HX + TX, rim_y_plane, zeros16)
+    acc = lax.fori_loop(HX, HX + TX, rim_y_plane, zeros16, unroll=2)
     for m in range(4):
         for n in range(4):
             line = jnp.sum(acc[4 * m + n], axis=0, keepdims=True)
@@ -326,7 +348,7 @@
             return tuple(acc)
 
         count = len(group) + (8 if last else 0)
-        acc = lax.fori_loop(0, TX, gather, tuple(jnp.zeros((8, 128), F32) for _ in range(count)))
+        acc = lax.fori_loop(0, TX, gather, tuple(jnp.zeros((8, 128), F32) for _ in range(count)), unroll=2)
         for n, (a, c) in enumerate(group):
             line = jnp.sum(acc[n], axis=0, keepdims=True)
             wide[c, a : a + 1, :] = line
@@ -334,7 +356,8 @@
                 wide[a, c : c + 1, :] = line
         if last:
             for a in range(8):
-                wide[16, a : a + 1, :] = jnp.sum(acc[len(group) + a], axis=0, keepdims=True)
+                at = (8, a) if a in edge4 else (9, a + 2)
+                wide[at[0], at[1] : at[1] + 1, :] = jnp.sum(acc[len(group) + a], axis=0, keepdims=True)
 
     def ranges(places):
         total = jnp.zeros((8, 128), F32)
@@ -346,40 +369,35 @@
             total = total + roll(line, 8 + slot)
         return total
 
-    mine[0:8, :] = ranges([(n, n) for n in range(8)] + [(8 + m, 8 + corner4[m]) for m in range(4)])
-    mine[8:16, :] = ranges([(12 + m, 2 * m) for m in range(4)] + [(16, 1)])
+    mine[...] = ranges(
+        [(n, n) for n in range(8)] + [(8 + m, 8 + corner4[m]) for m in range(4)] + [(12 + m, 8 + edge4[m]) for m in range(4)]
+    )
+    hear(2)
 
     def exchange(src, slots, send, recv, axis):
         me = gx if axis == 0 else gy
         size = DX if axis == 0 else DY
-        sent = []
         for d in range(1, size):
             to = ((gx + d) % DX, gy) if axis == 0 else (gx, (gy + d) % DY)
-            copy = pltpu.make_async_remote_copy(
-                src_ref=src, dst_ref=slots.at[me], send_sem=send.at[d], recv_sem=recv.at[d],
+            pltpu.make_async_remote_copy(
+                src_ref=src, dst_ref=slots.at[me], send_sem=send, recv_sem=recv,
                 device_id=to, device_id_type=MESH,
-            )
-            copy.start()
-            sent.append(copy)
+            ).start()
         slots[me] = src[...]
-        for copy in sent:
-            copy.wait_recv()
-        return sent
+        arrived = slots.at[pl.ds(0, size - 1)]
+        pltpu.make_async_copy(arrived, arrived, recv).wait()
+        return pltpu.make_async_copy(arrived, arrived, send)
 
     def tree(items):
         while len(items) > 1:
             items = [a + b for a, b in zip(items[::2], items[1::2])] + (items[-1:] if len(items) % 2 else [])
         return items[0]
 
-    sent = exchange(mine, stage1, xsend, xrecv, 0)
+    sent_x = exchange(mine, stage1, xsend, xrecv, 0)
     half[...] = tree([stage1[n] for n in range(DX)])
-    sent += exchange(half, stage2, ysend, yrecv, 1)
-
-    def parts(rows):
-        return [tree([stage2[n, rows : rows + 8, :] for n in range(*ends)]) for ends in ((0, 6), (6, 10), (10, 16))]
-
-    pa, pb, pc = parts(0)
-    qa, qb, qc = parts(8)
+    sent_y = exchange(half, stage2, ysend, yrecv, 1)
+
+    pa, pb, pc = [tree([stage2[n] for n in range(*ends)]) for ends in ((0, 6), (6, 10), (10, 16))]
     slot = lane % 16
     ly, sy = lane % 2, sub % 2
     lk, sk = lane // 2 % 2, sub // 2 % 2
@@ -392,7 +410,8 @@
 
     m00, m01 = (ly == 0) & (sy == 0), (ly == 0) & (sy == 1)
     m10, m11 = (ly == 1) & (sy == 0), (ly == 1) & (sy == 1)
-    pairs_y = (slot < 8) & (lk < 2)
+    qa, qb = [keep(slot % 4 == 0, roll(p, -10)) + keep(slot % 4 == 2, roll(p, -9)) for p in (pa, pb)]
+    pairs_y = slot < 8
     y01 = keep(pairs_y & m00, qa) + keep(pairs_y & m11, rows_up(roll(qb, 1), 1))
     y10 = keep(pairs_y & m00, rows_up(qa, -1)) + keep(pairs_y & m11, roll(qb, 1))
     joined = [[pa + keep(m11, pb), keep(m10, pb) + y01], [keep(m01, pb) + y10, pc + keep(m00, pb)]]
@@ -409,8 +428,11 @@
         return low + rows_up(high, 2) if pk == 0 else rows_up(low, -2) + high
 
     node = [[by_column(by_row[pk], pq) for pq in range(2)] for pk in range(2)]
-    loads = [qa + keep(sy == 1, qb), qc + keep(sy == 0, qb)]
-    load_of = [by_column(loads, pk) for pk in range(2)]
+    loads = [pa + keep(sy == 1, pb), pc + keep(sy == 0, pb)]
+    load_of = [
+        keep(sk == 0, rows_up(roll(loads[0], -8), -2)) + keep(sk == 1, roll(loads[1], -8)),
+        rows_up(keep(sk == 1, roll(loads[0], -7)), -2) + keep(sk == 1, roll(loads[1], -7)),
+    ]
     layer = lane // 16
     even = layer % 2 == 0
     own = jnp.where(even, node[0][0] + roll(node[0][0], -16), node[1][1] + roll(node[1][1], -16))
@@ -547,20 +569,24 @@
         j = jnp.clip(j, 0, 3)
         return val[pz, pl.ds(4 * px + j, 1), :]
 
-    for t in range(4):
-        tile = gy + (-1, 0, 0, 1)[t]
-        weights = [jnp.broadcast_to(node_row(px, py, pz, tile), (8, 128)) for px, py, pz in COLORS]
-
-        def prolong(x, _, t=t, weights=weights):
-            prol[x, 8 * t : 8 * t + 8, :] = functools.reduce(
-                jnp.add, [weights[c] * basis[c, x, 8 * t : 8 * t + 8, :] for c in range(8)]
+    before, here, beyond = [[node_row(px, py, pz, gy + d) for px, py, pz in COLORS] for d in (-1, 0, 1)]
+    for t in range(3):
+        r = HY - 1 + 8 * t
+        first, others = ((before, here), (here, here), (here, beyond))[t]
+        weights = [jnp.where(sub == 0, a, b) for a, b in zip(first, others)]
+
+        def prolong(x, _, r=r, weights=weights):
+            prol[x, r : r + 8, :] = functools.reduce(
+                jnp.add, [weights[c] * basis[c, x, r : r + 8, :] for c in range(8)]
             )
             return 0
 
-        lax.fori_loop(HX - 1, HX + TX + 1, prolong, 0)
-
-    for copy in copies + sent:
+        lax.fori_loop(HX - 1, HX + TX + 1, prolong, 0, unroll=5)
+
+    for copy in copies:
         copy.wait_send()
+    sent_x.wait()
+    sent_y.wait()
 
     def finish(x, _):
         for t in range(2):
@@ -575,7 +601,7 @@
             out_ref[x - HX, 8 * t : 8 * t + 8, :] = v + wdiag[x, r : r + 8, :] * (load - q)
         return 0
 
-    lax.fori_loop(HX, HX + TX, finish, 0)
+    lax.fori_loop(HX, HX + TX, finish, 0, unroll=2)
 
 
 def per_device(facies, source, facies_perm, facies_store, well_x, well_y, well_rate):
@@ -602,13 +628,13 @@
             pltpu.VMEM((8, TX, TY, 128), F32),
             pltpu.VMEM((8, TX, TY, 128), F32),
             pltpu.VMEM((TX, TY, 128), F32),
-            pltpu.VMEM((17, 8, 128), F32),
-            pltpu.VMEM((DX, 16, 128), F32),
-            pltpu.VMEM((DY, 16, 128), F32),
+            pltpu.VMEM((16, 8, 128), F32),
+            pltpu.VMEM((DX, 8, 128), F32),
+            pltpu.VMEM((DY, 8, 128), F32),
             pltpu.VMEM((2, 8, 128), F32),
             field,
-            pltpu.VMEM((16, 128), F32),
-            pltpu.VMEM((16, 128), F32),
+            pltpu.VMEM((8, 128), F32),
+            pltpu.VMEM((8, 128), F32),
             pltpu.VMEM((TX, TY, 128), F32),
             pltpu.VMEM((1, WELLS), jnp.int32),
             pltpu.VMEM((1, WELLS), jnp.int32),
@@ -616,10 +642,12 @@
             pltpu.SemaphoreType.DMA((5,)),
             pltpu.SemaphoreType.DMA((8,)),
             pltpu.SemaphoreType.DMA((8,)),
-            pltpu.SemaphoreType.DMA((DX,)),
-            pltpu.SemaphoreType.DMA((DX,)),
-            pltpu.SemaphoreType.DMA((DY,)),
-            pltpu.SemaphoreType.DMA((DY,)),
+            pltpu.SemaphoreType.DMA,
+            pltpu.SemaphoreType.DMA,
+            pltpu.SemaphoreType.DMA,
+            pltpu.SemaphoreType.DMA,
+            pltpu.SemaphoreType.REGULAR((3,)),
+            pltpu.SemaphoreType.REGULAR((3,)),
         ],
         compiler_params=pltpu.CompilerParams(
             collective_id=0, has_side_effects=True, vmem_limit_bytes=40 * 1024 * 1024

time: 46.1 us -> 38.6 us (0.84)
  Pallas kernels: 42.9 us -> 35.4 us
    pallas_call x1, Pallas kernels: 42.9 us -> 35.4 us  [per_device(): pl.pallas_call(kernel, out_shape=jax.ShapeDtypeStruct((TX, TY, CELLS_Z),...]
where the time goes in v3:
time: 38.6 us; the launch traced here: 38.5 us
  Pallas kernels  35.4 us (92%)
  local copies, waits for them, and re-layouts  3.01 us (8%)
    pallas_call x1, Pallas kernels, per_device(): pl.pallas_call(kernel, out_shape=jax.ShapeDtypeStruct((TX, TY, CELLS_Z),...  35.4 us
    unnamed x15, local copies, waits for them, and re-layouts  3.01 us

profile of v3, /device:TPU:1, one launch (start us, length us, event | category | flops | bytes accessed | tf_op | source)
XLA Modules:
  0.0 38.5 jit_solution(4674102568626560306)
XLA Ops:
  0.0 0.0 copy-start.5
  0.0 0.0 copy-start.6
  0.0 0.0 copy-start.2
  0.0 0.0 copy-start.3
  0.0 0.0 copy-start.4
  0.0 0.6 %copy-done.5 = s32[64]{0:T(128)S(1)} copy-done((s32[64]{0:T(128)S(1)}, s32[64]{0:T(128)}, u32[]{:S(2)}) %copy-start.5) | copy-done | bytes 280
  0.7 0.0 copy-done.6
  0.7 0.0 copy-done.2
  0.7 0.0 copy-done.3
  0.7 0.0 copy-done.4
  0.7 0.0 copy-start
  0.7 0.8 %copy-done = s32[8,16,128]{2,1,0:T(8,128)S(1)} copy-done((s32[8,16,128]{2,1,0:T(8,128)S(1)}, s32[8,16,128]{2,1,0:T(8,128)}, u32[]{:S(2)}) %copy-start) | copy-done | bytes 65560
  1.6 0.0 copy-start.1
  1.6 0.8 %copy-done.1 = f32[8,16,128]{2,1,0:T(8,128)S(1)} copy-done((f32[8,16,128]{2,1,0:T(8,128)S(1)}, f32[8,16,128]{2,1,0:T(8,128)}, u32[]{:S(2)}) %copy-start.1) | copy-done | bytes 65560
  2.4 35.4 %shard_map.73 = f32[8,16,128]{2,1,0:T(8,128)S(1)} custom-call(s32[8,16,128]{2,1,0:T(8,128)S(1)} %copy-done, f32[8,16,128]{2,1,0:T(8,128)S(1)} %copy-done.1, f32[8]{0:T(128)S(1)} %copy-done.2, f32[8]{0:T(128)S(1)} %copy-done.3, s32[1,64]{1,0:T(1,128)S(1)} %bitcast.3, s32[1,64]{1,0:T(1,128)S(1)} %bitcast.4, f32[1,64]{1,0:T(1,128)S(1)} %bitcast.5), custom_call_target="tpu_custom_call" | custom-call | tf_op jit(solution)/shard_map/pallas_call | solution.py:613
  37.8 0.6 %copy.9 = f32[8,16,128]{2,1,0:T(8,128)} copy(f32[8,16,128]{2,1,0:T(8,128)S(1)} %shard_map.73) | data formatting | bytes 131072
Async XLA Ops:
  0.0 0.7 %copy-start.5 = (s32[64]{0:T(128)S(1)}, s32[64]{0:T(128)}, u32[]{:S(2)}) copy-start(s32[64]{0:T(128)} %param.12) | copy-start | bytes 772
  0.0 0.7 %copy-start.6 = (f32[64]{0:T(128)S(1)}, f32[64]{0:T(128)}, u32[]{:S(2)}) copy-start(f32[64]{0:T(128)} %param.13) | copy-start | bytes 772
  0.0 0.7 %copy-start.2 = (f32[8]{0:T(128)S(1)}, f32[8]{0:T(128)}, u32[]{:S(2)}) copy-start(f32[8]{0:T(128)} %perm_ref.1) | copy-start | bytes 100
  0.0 0.7 %copy-start.3 = (f32[8]{0:T(128)S(1)}, f32[8]{0:T(128)}, u32[]{:S(2)}) copy-start(f32[8]{0:T(128)} %store_ref.1) | copy-start | bytes 100
  0.0 0.7 %copy-start.4 = (s32[64]{0:T(128)S(1)}, s32[64]{0:T(128)}, u32[]{:S(2)}) copy-start(s32[64]{0:T(128)} %param.11) | copy-start | bytes 772
  0.7 0.8 %copy-start = (s32[8,16,128]{2,1,0:T(8,128)S(1)}, s32[8,16,128]{2,1,0:T(8,128)}, u32[]{:S(2)}) copy-start(s32[8,16,128]{2,1,0:T(8,128)} %facies_hbm.1) | copy-start | bytes 196612
  1.6 0.8 %copy-start.1 = (f32[8,16,128]{2,1,0:T(8,128)S(1)}, f32[8,16,128]{2,1,0:T(8,128)}, u32[]{:S(2)}) copy-start(f32[8,16,128]{2,1,0:T(8,128)} %source_hbm.1) | copy-start | bytes 196612

commit v4 on v3

--- a/solution.py
+++ b/solution.py
@@ -52,7 +52,7 @@
     facies_hbm, source_hbm, perm_ref, store_ref, wx_hbm, wy_hbm, wr_hbm, out_ref,
     fac, hperm, stor, coef, trans, wdiag, va, vb, bv, rim, rimy, rhs, wide, stage1, stage2, val, prol,
     mine, half, source_ref, wx_ref, wy_ref, wr_ref,
-    insem, hsend, hrecv, xsend, xrecv, ysend, yrecv, news_x, news_y,
+    insem, hsend, hrecv, xsend, xrecv, ysend, yrecv, news,
 ):
     gx = lax.axis_index("gx")
     gy = lax.axis_index("gy")
@@ -67,49 +67,37 @@
         pltpu.make_async_copy(wr_hbm, wr_ref, insem.at[4]),
     ]
     barrier = pltpu.get_barrier_semaphore()
-    near = [((gx + i) % DX, (gy + j) % DY) for i in (0, 1, DX - 1) for j in (0, 1, DY - 1) if i or j]
-    for who in near:
+    diagonal = [((gx + i) % DX, (gy + j) % DY) for i in (1, DX - 1) for j in (1, DY - 1)]
+    known = [((gx + d) % DX, gy) for d in (1, DX - 1, 3, DX - 3, 8)] + [(gx, (gy + d) % DY) for d in (1, DY - 1, 3, DY - 3, 8)]
+    for who in diagonal + known:
         pl.semaphore_signal(barrier, inc=1, device_id=who, device_id_type=MESH)
     for copy in inputs:
         copy.start()
-    pl.semaphore_wait(barrier, len(near))
-
-    def tell(n):
-        d = 1 << n
-        for i in (d, DX - d):
-            pl.semaphore_signal(news_x.at[n], inc=1, device_id=((gx + i) % DX, gy), device_id_type=MESH)
-        for j in (d, DY - d):
-            pl.semaphore_signal(news_y.at[n], inc=1, device_id=(gx, (gy + j) % DY), device_id_type=MESH)
-
-    def hear(n):
-        pl.semaphore_wait(news_x.at[n], 2)
-        pl.semaphore_wait(news_y.at[n], 2)
+    pl.semaphore_wait(barrier, len(diagonal) + len(known))
 
     copies = []
     n = 0
-    for dx in (-1, 0, 1):
-        for dy in (-1, 0, 1):
-            if dx == 0 and dy == 0:
-                continue
-            wx = HX if dy == 0 else HX - 1
-            sx = {1: (TX - wx, wx), -1: (0, wx), 0: (0, TX)}[dx]
-            sy = {1: (TY - 4, 4), -1: (0, 4), 0: (0, TY)}[dy]
-            tx = {1: HX - wx, -1: HX + TX, 0: HX}[dx]
-            ty = {1: HY - 4, -1: HY + TY, 0: HY}[dy]
-            copies.append(
-                pltpu.make_async_remote_copy(
-                    src_ref=facies_hbm.at[pl.ds(sx[0], sx[1]), pl.ds(sy[0], sy[1])],
-                    dst_ref=fac.at[pl.ds(tx, sx[1]), pl.ds(ty, sy[1])],
-                    send_sem=hsend.at[n],
-                    recv_sem=hrecv.at[n],
-                    device_id=((gx + dx + DX) % DX, (gy + dy + DY) % DY),
-                    device_id_type=MESH,
-                )
+    for dx, dy in ((-1, -1), (-1, 1), (1, -1), (1, 1), (-1, 0), (1, 0), (0, -1), (0, 1)):
+        wx = HX if dy == 0 else HX - 1
+        sx = {1: (TX - wx, wx), -1: (0, wx), 0: (0, TX)}[dx]
+        sy = {1: (TY - 4, 4), -1: (0, 4), 0: (0, TY)}[dy]
+        tx = {1: HX - wx, -1: HX + TX, 0: HX}[dx]
+        ty = {1: HY - 4, -1: HY + TY, 0: HY}[dy]
+        copies.append(
+            pltpu.make_async_remote_copy(
+                src_ref=facies_hbm.at[pl.ds(sx[0], sx[1]), pl.ds(sy[0], sy[1])],
+                dst_ref=fac.at[pl.ds(tx, sx[1]), pl.ds(ty, sy[1])],
+                send_sem=hsend.at[n],
+                recv_sem=hrecv.at[n],
+                device_id=((gx + dx + DX) % DX, (gy + dy + DY) % DY),
+                device_id_type=MESH,
             )
-            n += 1
+        )
+        n += 1
     for copy in copies:
         copy.start()
-    tell(0)
+    for who in known:
+        pl.semaphore_signal(news, inc=1, device_id=who, device_id_type=MESH)
 
     for copy in inputs[1:]:
         copy.wait()
@@ -167,14 +155,9 @@
         return plane
 
     lax.fori_loop(HX, HX + TX, lookup((1, 2)), 0)
-    for copy in copies:
+    for copy in copies[6:]:
         copy.wait_recv()
-    lax.fori_loop(0, HX, lookup(range(4)), 0)
     lax.fori_loop(HX, HX + TX, lookup((0, 3)), 0)
-    lax.fori_loop(HX + TX, EX, lookup(range(4)), 0)
-
-    hear(0)
-    tell(1)
 
     def coef_plane(x, _):
         gxe = ax - HX + x
@@ -205,9 +188,8 @@
                 coef[10 + p, x, a : a + 8, :] = wzp * same_zp[p]
         return 0
 
-    lax.fori_loop(1, EX - 1, coef_plane, 0, unroll=UNROLL_COEF)
-
-    def sweep(src, dst, low):
+
+    def sweep(src, dst, *spans):
         def plane(x, _):
             for t in range(3):
                 r, a = 4 + 8 * t, 8 * t
@@ -226,13 +208,22 @@
                     dst[c, x, r : r + 8, :] = new[c] + old[c] * keep
             return 0
 
-        lax.fori_loop(low, EX - low, plane, 0, unroll=UNROLL_SWEEP)
-
-    sweep(va, vb, 1)
-    hear(1)
-    tell(2)
-    sweep(vb, va, 2)
-    sweep(va, vb, 3)
+        for span in spans:
+            lax.fori_loop(*span, plane, 0, unroll=UNROLL_SWEEP)
+
+    lax.fori_loop(5, 11, coef_plane, 0, unroll=UNROLL_COEF)
+    sweep(va, vb, (5, 11))
+    sweep(vb, va, (6, 10))
+    sweep(va, vb, (7, 9))
+    for copy in copies[:6]:
+        copy.wait_recv()
+    lax.fori_loop(0, HX, lookup(range(4)), 0, unroll=2)
+    lax.fori_loop(HX + TX, EX, lookup(range(4)), 0, unroll=2)
+    lax.fori_loop(1, 5, coef_plane, 0, unroll=UNROLL_COEF)
+    lax.fori_loop(11, 15, coef_plane, 0, unroll=UNROLL_COEF)
+    sweep(va, vb, (1, 5), (11, 15))
+    sweep(vb, va, (2, 6), (10, 14))
+    sweep(va, vb, (3, 7), (9, 13))
     basis = vb
 
     tile_rows = [ay + 8 * t + sub for t in range(2)]
@@ -372,7 +363,7 @@
     mine[...] = ranges(
         [(n, n) for n in range(8)] + [(8 + m, 8 + corner4[m]) for m in range(4)] + [(12 + m, 8 + edge4[m]) for m in range(4)]
     )
-    hear(2)
+    pl.semaphore_wait(news, len(known))
 
     def exchange(src, slots, send, recv, axis):
         me = gx if axis == 0 else gy
@@ -646,8 +637,7 @@
             pltpu.SemaphoreType.DMA,
             pltpu.SemaphoreType.DMA,
             pltpu.SemaphoreType.DMA,
-            pltpu.SemaphoreType.REGULAR((3,)),
-            pltpu.SemaphoreType.REGULAR((3,)),
+            pltpu.SemaphoreType.REGULAR,
         ],
         compiler_params=pltpu.CompilerParams(
             collective_id=0, has_side_effects=True, vmem_limit_bytes=40 * 1024 * 1024

time: 38.6 us -> 36.4 us (0.943)
  Pallas kernels: 35.4 us -> 33.2 us
    pallas_call x1, Pallas kernels: 35.4 us -> 33.2 us  [per_device(): pl.pallas_call(kernel, out_shape=jax.ShapeDtypeStruct((TX, TY, CELLS_Z),...]
where the time goes in v4:
time: 36.4 us; the launch traced here: 36.3 us
  Pallas kernels  33.2 us (91%)
  local copies, waits for them, and re-layouts  3.01 us (8%)
    pallas_call x1, Pallas kernels, per_device(): pl.pallas_call(kernel, out_shape=jax.ShapeDtypeStruct((TX, TY, CELLS_Z),...  33.2 us
    unnamed x15, local copies, waits for them, and re-layouts  3.01 us

profile of v4, /device:TPU:1, one launch (start us, length us, event | category | flops | bytes accessed | tf_op | source)
XLA Modules:
  0.0 36.3 jit_solution(9321544368305407669)
XLA Ops:
  0.0 0.0 copy-start.5
  0.0 0.0 copy-start.6
  0.0 0.0 copy-start.2
  0.0 0.0 copy-start.3
  0.0 0.0 copy-start.4
  0.0 0.6 %copy-done.5 = s32[64]{0:T(128)S(1)} copy-done((s32[64]{0:T(128)S(1)}, s32[64]{0:T(128)}, u32[]{:S(2)}) %copy-start.5) | copy-done | bytes 280
  0.7 0.0 copy-done.6
  0.7 0.0 copy-done.2
  0.7 0.0 copy-done.3
  0.7 0.0 copy-done.4
  0.7 0.0 copy-start
  0.7 0.8 %copy-done = s32[8,16,128]{2,1,0:T(8,128)S(1)} copy-done((s32[8,16,128]{2,1,0:T(8,128)S(1)}, s32[8,16,128]{2,1,0:T(8,128)}, u32[]{:S(2)}) %copy-start) | copy-done | bytes 65560
  1.6 0.0 copy-start.1
  1.6 0.8 %copy-done.1 = f32[8,16,128]{2,1,0:T(8,128)S(1)} copy-done((f32[8,16,128]{2,1,0:T(8,128)S(1)}, f32[8,16,128]{2,1,0:T(8,128)}, u32[]{:S(2)}) %copy-start.1) | copy-done | bytes 65560
  2.4 33.2 %shard_map.73 = f32[8,16,128]{2,1,0:T(8,128)S(1)} custom-call(s32[8,16,128]{2,1,0:T(8,128)S(1)} %copy-done, f32[8,16,128]{2,1,0:T(8,128)S(1)} %copy-done.1, f32[8]{0:T(128)S(1)} %copy-done.2, f32[8]{0:T(128)S(1)} %copy-done.3, s32[1,64]{1,0:T(1,128)S(1)} %bitcast.3, s32[1,64]{1,0:T(1,128)S(1)} %bitcast.4, f32[1,64]{1,0:T(1,128)S(1)} %bitcast.5), custom_call_target="tpu_custom_call" | custom-call | tf_op jit(solution)/shard_map/pallas_call | solution.py:604
  35.6 0.6 %copy.9 = f32[8,16,128]{2,1,0:T(8,128)} copy(f32[8,16,128]{2,1,0:T(8,128)S(1)} %shard_map.73) | data formatting | bytes 131072
Async XLA Ops:
  0.0 0.7 %copy-start.5 = (s32[64]{0:T(128)S(1)}, s32[64]{0:T(128)}, u32[]{:S(2)}) copy-start(s32[64]{0:T(128)} %param.12) | copy-start | bytes 772
  0.0 0.7 %copy-start.6 = (f32[64]{0:T(128)S(1)}, f32[64]{0:T(128)}, u32[]{:S(2)}) copy-start(f32[64]{0:T(128)} %param.13) | copy-start | bytes 772
  0.0 0.7 %copy-start.2 = (f32[8]{0:T(128)S(1)}, f32[8]{0:T(128)}, u32[]{:S(2)}) copy-start(f32[8]{0:T(128)} %perm_ref.1) | copy-start | bytes 100
  0.0 0.7 %copy-start.3 = (f32[8]{0:T(128)S(1)}, f32[8]{0:T(128)}, u32[]{:S(2)}) copy-start(f32[8]{0:T(128)} %store_ref.1) | copy-start | bytes 100
  0.0 0.7 %copy-start.4 = (s32[64]{0:T(128)S(1)}, s32[64]{0:T(128)}, u32[]{:S(2)}) copy-start(s32[64]{0:T(128)} %param.11) | copy-start | bytes 772
  0.7 0.8 %copy-start = (s32[8,16,128]{2,1,0:T(8,128)S(1)}, s32[8,16,128]{2,1,0:T(8,128)}, u32[]{:S(2)}) copy-start(s32[8,16,128]{2,1,0:T(8,128)} %facies_hbm.1) | copy-start | bytes 196612
  1.6 0.8 %copy-start.1 = (f32[8,16,128]{2,1,0:T(8,128)S(1)}, f32[8,16,128]{2,1,0:T(8,128)}, u32[]{:S(2)}) copy-start(f32[8,16,128]{2,1,0:T(8,128)} %source_hbm.1) | copy-start | bytes 196612

commit v5 on v4

--- a/solution.py
+++ b/solution.py
@@ -18,7 +18,7 @@
 EX, EY = TX + 2 * HX, TY + 2 * HY
 DX, DY = 16, 16
 MESH = pl.DeviceIdType.MESH
-UNROLL_SWEEP, UNROLL_COEF = True, 2
+UNROLL_SWEEP, UNROLL_COEF = True, True
 F32 = jnp.float32
 
 COLORS = [(c >> 2 & 1, c & 1, c >> 1 & 1) for c in range(8)]
@@ -154,10 +154,10 @@
 
         return plane
 
-    lax.fori_loop(HX, HX + TX, lookup((1, 2)), 0)
+    lax.fori_loop(HX, HX + TX, lookup((1, 2)), 0, unroll=2)
     for copy in copies[6:]:
         copy.wait_recv()
-    lax.fori_loop(HX, HX + TX, lookup((0, 3)), 0)
+    lax.fori_loop(HX, HX + TX, lookup((0, 3)), 0, unroll=True)
 
     def coef_plane(x, _):
         gxe = ax - HX + x
@@ -217,8 +217,8 @@
     sweep(va, vb, (7, 9))
     for copy in copies[:6]:
         copy.wait_recv()
-    lax.fori_loop(0, HX, lookup(range(4)), 0, unroll=2)
-    lax.fori_loop(HX + TX, EX, lookup(range(4)), 0, unroll=2)
+    lax.fori_loop(0, HX, lookup(range(4)), 0, unroll=True)
+    lax.fori_loop(HX + TX, EX, lookup(range(4)), 0, unroll=True)
     lax.fori_loop(1, 5, coef_plane, 0, unroll=UNROLL_COEF)
     lax.fori_loop(11, 15, coef_plane, 0, unroll=UNROLL_COEF)
     sweep(va, vb, (1, 5), (11, 15))
@@ -250,7 +250,7 @@
                 )
         return 0
 
-    lax.fori_loop(HX, HX + TX, apply_plane, 0, unroll=2)
+    lax.fori_loop(HX, HX + TX, apply_plane, 0, unroll=True)
 
     west = lane < 64
     cut_lo = [1.0 - same_z(lane, p) for p in range(2)]
@@ -279,7 +279,7 @@
         return tuple(acc)
 
     zeros16 = tuple(jnp.zeros((8, 128), F32) for _ in range(16))
-    acc = lax.fori_loop(HX, HX + TX, rim_plane, zeros16, unroll=2)
+    acc = lax.fori_loop(HX, HX + TX, rim_plane, zeros16, unroll=True)
     for n in range(8, 12):
         wide[n] = jnp.zeros((8, 128), F32)
     corner4, edge4 = (0, 1, 4, 5), (2, 3, 6, 7)
@@ -301,7 +301,7 @@
                 acc[4 * m + n] = acc[4 * m + n] + here[m] * there[n]
         return tuple(acc)
 
-    acc = lax.fori_loop(HX, HX + TX, rim_y_plane, zeros16, unroll=2)
+    acc = lax.fori_loop(HX, HX + TX, rim_y_plane, zeros16, unroll=True)
     for m in range(4):
         for n in range(4):
             line = jnp.sum(acc[4 * m + n], axis=0, keepdims=True)
@@ -339,7 +339,7 @@
             return tuple(acc)
 
         count = len(group) + (8 if last else 0)
-        acc = lax.fori_loop(0, TX, gather, tuple(jnp.zeros((8, 128), F32) for _ in range(count)), unroll=2)
+        acc = lax.fori_loop(0, TX, gather, tuple(jnp.zeros((8, 128), F32) for _ in range(count)), unroll=True)
         for n, (a, c) in enumerate(group):
             line = jnp.sum(acc[n], axis=0, keepdims=True)
             wide[c, a : a + 1, :] = line
@@ -592,7 +592,7 @@
             out_ref[x - HX, 8 * t : 8 * t + 8, :] = v + wdiag[x, r : r + 8, :] * (load - q)
         return 0
 
-    lax.fori_loop(HX, HX + TX, finish, 0, unroll=2)
+    lax.fori_loop(HX, HX + TX, finish, 0, unroll=True)
 
 
 def per_device(facies, source, facies_perm, facies_store, well_x, well_y, well_rate):

time: 36.4 us -> 35.7 us (0.981)
  Pallas kernels: 33.2 us -> 32.5 us
    pallas_call x1, Pallas kernels: 33.2 us -> 32.5 us  [per_device(): pl.pallas_call(kernel, out_shape=jax.ShapeDtypeStruct((TX, TY, CELLS_Z),...]
where the time goes in v5:
time: 35.7 us; the launch traced here: 35.5 us
  Pallas kernels  32.5 us (91%)
  local copies, waits for them, and re-layouts  3.01 us (8%)
    pallas_call x1, Pallas kernels, per_device(): pl.pallas_call(kernel, out_shape=jax.ShapeDtypeStruct((TX, TY, CELLS_Z),...  32.5 us
    unnamed x15, local copies, waits for them, and re-layouts  3.01 us

profile of v5, /device:TPU:1, one launch (start us, length us, event | category | flops | bytes accessed | tf_op | source)
XLA Modules:
  0.0 35.5 jit_solution(12116255705665468080)
XLA Ops:
  0.0 0.0 copy-start.5
  0.0 0.0 copy-start.6
  0.0 0.0 copy-start.2
  0.0 0.0 copy-start.3
  0.0 0.0 copy-start.4
  0.0 0.6 %copy-done.5 = s32[64]{0:T(128)S(1)} copy-done((s32[64]{0:T(128)S(1)}, s32[64]{0:T(128)}, u32[]{:S(2)}) %copy-start.5) | copy-done | bytes 280
  0.7 0.0 copy-done.6
  0.7 0.0 copy-done.2
  0.7 0.0 copy-done.3
  0.7 0.0 copy-done.4
  0.7 0.0 copy-start
  0.7 0.8 %copy-done = s32[8,16,128]{2,1,0:T(8,128)S(1)} copy-done((s32[8,16,128]{2,1,0:T(8,128)S(1)}, s32[8,16,128]{2,1,0:T(8,128)}, u32[]{:S(2)}) %copy-start) | copy-done | bytes 65560
  1.6 0.0 copy-start.1
  1.6 0.8 %copy-done.1 = f32[8,16,128]{2,1,0:T(8,128)S(1)} copy-done((f32[8,16,128]{2,1,0:T(8,128)S(1)}, f32[8,16,128]{2,1,0:T(8,128)}, u32[]{:S(2)}) %copy-start.1) | copy-done | bytes 65560
  2.4 32.5 %shard_map.73 = f32[8,16,128]{2,1,0:T(8,128)S(1)} custom-call(s32[8,16,128]{2,1,0:T(8,128)S(1)} %copy-done, f32[8,16,128]{2,1,0:T(8,128)S(1)} %copy-done.1, f32[8]{0:T(128)S(1)} %copy-done.2, f32[8]{0:T(128)S(1)} %copy-done.3, s32[1,64]{1,0:T(1,128)S(1)} %bitcast.3, s32[1,64]{1,0:T(1,128)S(1)} %bitcast.4, f32[1,64]{1,0:T(1,128)S(1)} %bitcast.5), custom_call_target="tpu_custom_call" | custom-call | tf_op jit(solution)/shard_map/pallas_call | solution.py:604
  34.9 0.6 %copy.9 = f32[8,16,128]{2,1,0:T(8,128)} copy(f32[8,16,128]{2,1,0:T(8,128)S(1)} %shard_map.73) | data formatting | bytes 131072
Async XLA Ops:
  0.0 0.7 %copy-start.5 = (s32[64]{0:T(128)S(1)}, s32[64]{0:T(128)}, u32[]{:S(2)}) copy-start(s32[64]{0:T(128)} %param.12) | copy-start | bytes 772
  0.0 0.7 %copy-start.6 = (f32[64]{0:T(128)S(1)}, f32[64]{0:T(128)}, u32[]{:S(2)}) copy-start(f32[64]{0:T(128)} %param.13) | copy-start | bytes 772
  0.0 0.7 %copy-start.2 = (f32[8]{0:T(128)S(1)}, f32[8]{0:T(128)}, u32[]{:S(2)}) copy-start(f32[8]{0:T(128)} %perm_ref.1) | copy-start | bytes 100
  0.0 0.7 %copy-start.3 = (f32[8]{0:T(128)S(1)}, f32[8]{0:T(128)}, u32[]{:S(2)}) copy-start(f32[8]{0:T(128)} %store_ref.1) | copy-start | bytes 100
  0.0 0.7 %copy-start.4 = (s32[64]{0:T(128)S(1)}, s32[64]{0:T(128)}, u32[]{:S(2)}) copy-start(s32[64]{0:T(128)} %param.11) | copy-start | bytes 772
  0.7 0.8 %copy-start = (s32[8,16,128]{2,1,0:T(8,128)S(1)}, s32[8,16,128]{2,1,0:T(8,128)}, u32[]{:S(2)}) copy-start(s32[8,16,128]{2,1,0:T(8,128)} %facies_hbm.1) | copy-start | bytes 196612
  1.6 0.8 %copy-start.1 = (f32[8,16,128]{2,1,0:T(8,128)S(1)}, f32[8,16,128]{2,1,0:T(8,128)}, u32[]{:S(2)}) copy-start(f32[8,16,128]{2,1,0:T(8,128)} %source_hbm.1) | copy-start | bytes 196612

commit v6 on v5

--- a/solution.py
+++ b/solution.py
@@ -155,43 +155,43 @@
         return plane
 
     lax.fori_loop(HX, HX + TX, lookup((1, 2)), 0, unroll=2)
-    for copy in copies[6:]:
-        copy.wait_recv()
-    lax.fori_loop(HX, HX + TX, lookup((0, 3)), 0, unroll=True)
-
-    def coef_plane(x, _):
-        gxe = ax - HX + x
-        ok_m = flag(inside(gxe - 1, GRID_X) & inside(gxe, GRID_X))
-        ok_p = flag(inside(gxe, GRID_X) & inside(gxe + 1, GRID_X))
-        for t in range(3):
-            r = 4 + 8 * t
-            h = hperm[x, r : r + 8, :]
-            txm = ok_m / (h + hperm[x - 1, r : r + 8, :])
-            txp = ok_p / (h + hperm[x + 1, r : r + 8, :])
-            tym = row_m[t] / (h + hperm[x, r - 1 : r + 7, :])
-            typ = row_p[t] / (h + hperm[x, r + 1 : r + 9, :])
-            tzp = last_z / (h + roll(h, -1))
-            tzm = roll(tzp, 1)
-            diag = stor[x, r : r + 8, :] + txm + txp + tym + typ + tzm + tzp
-            w = RELAX / diag
-            wdiag[x, r : r + 8, :] = w
-            for n, value in enumerate((txm, txp, tym, typ, tzm, tzp)):
-                trans[n, x, r : r + 8, :] = value
-            wxm, wxp, wym, wyp, wzm, wzp = [w * v for v in (txm, txp, tym, typ, tzm, tzp)]
-            a = 8 * t
-            for p in range(2):
-                coef[p, x, a : a + 8, :] = wxm * same_xy(gxe - 1, p, BLOCK_X)
-                coef[2 + p, x, a : a + 8, :] = wxp * same_xy(gxe, p, BLOCK_X)
-                coef[4 + p, x, a : a + 8, :] = wym * same_ym[t][p]
-                coef[6 + p, x, a : a + 8, :] = wyp * same_yp[t][p]
-                coef[8 + p, x, a : a + 8, :] = wzm * same_zm[p]
-                coef[10 + p, x, a : a + 8, :] = wzp * same_zp[p]
-        return 0
-
-
-    def sweep(src, dst, *spans):
+
+    def coefficients(tiles, *spans):
+        def coef_plane(x, _):
+            gxe = ax - HX + x
+            ok_m = flag(inside(gxe - 1, GRID_X) & inside(gxe, GRID_X))
+            ok_p = flag(inside(gxe, GRID_X) & inside(gxe + 1, GRID_X))
+            for t in tiles:
+                r = 4 + 8 * t
+                h = hperm[x, r : r + 8, :]
+                txm = ok_m / (h + hperm[x - 1, r : r + 8, :])
+                txp = ok_p / (h + hperm[x + 1, r : r + 8, :])
+                tym = row_m[t] / (h + hperm[x, r - 1 : r + 7, :])
+                typ = row_p[t] / (h + hperm[x, r + 1 : r + 9, :])
+                tzp = last_z / (h + roll(h, -1))
+                tzm = roll(tzp, 1)
+                diag = stor[x, r : r + 8, :] + txm + txp + tym + typ + tzm + tzp
+                w = RELAX / diag
+                wdiag[x, r : r + 8, :] = w
+                for n, value in enumerate((txm, txp, tym, typ, tzm, tzp)):
+                    trans[n, x, r : r + 8, :] = value
+                wxm, wxp, wym, wyp, wzm, wzp = [w * v for v in (txm, txp, tym, typ, tzm, tzp)]
+                a = 8 * t
+                for p in range(2):
+                    coef[p, x, a : a + 8, :] = wxm * same_xy(gxe - 1, p, BLOCK_X)
+                    coef[2 + p, x, a : a + 8, :] = wxp * same_xy(gxe, p, BLOCK_X)
+                    coef[4 + p, x, a : a + 8, :] = wym * same_ym[t][p]
+                    coef[6 + p, x, a : a + 8, :] = wyp * same_yp[t][p]
+                    coef[8 + p, x, a : a + 8, :] = wzm * same_zm[p]
+                    coef[10 + p, x, a : a + 8, :] = wzp * same_zp[p]
+            return 0
+
+        for span in spans:
+            lax.fori_loop(*span, coef_plane, 0, unroll=UNROLL_COEF)
+
+    def sweep(src, dst, *spans, tiles=(0, 1, 2)):
         def plane(x, _):
-            for t in range(3):
+            for t in tiles:
                 r, a = 4 + 8 * t, 8 * t
                 k = [coef[n, x, a : a + 8, :] for n in range(12)]
                 old, new = [], []
@@ -211,17 +211,28 @@
         for span in spans:
             lax.fori_loop(*span, plane, 0, unroll=UNROLL_SWEEP)
 
-    lax.fori_loop(5, 11, coef_plane, 0, unroll=UNROLL_COEF)
-    sweep(va, vb, (5, 11))
+    inner, outer = (5, 11), ((1, 5), (11, 15))
+    coefficients((1,), inner)
+    sweep(va, vb, inner, tiles=(1,))
+    for copy in copies[6:]:
+        copy.wait_recv()
+    lax.fori_loop(HX, HX + TX, lookup((0, 3)), 0, unroll=True)
+    coefficients((0, 2), inner)
+    sweep(va, vb, inner, tiles=(0, 2))
     sweep(vb, va, (6, 10))
     sweep(va, vb, (7, 9))
-    for copy in copies[:6]:
+    for copy in copies[4:6]:
         copy.wait_recv()
-    lax.fori_loop(0, HX, lookup(range(4)), 0, unroll=True)
-    lax.fori_loop(HX + TX, EX, lookup(range(4)), 0, unroll=True)
-    lax.fori_loop(1, 5, coef_plane, 0, unroll=UNROLL_COEF)
-    lax.fori_loop(11, 15, coef_plane, 0, unroll=UNROLL_COEF)
-    sweep(va, vb, (1, 5), (11, 15))
+    for span in ((0, HX), (HX + TX, EX)):
+        lax.fori_loop(*span, lookup((1, 2)), 0, unroll=True)
+    coefficients((1,), *outer)
+    sweep(va, vb, *outer, tiles=(1,))
+    for copy in copies[:4]:
+        copy.wait_recv()
+    for span in ((0, HX), (HX + TX, EX)):
+        lax.fori_loop(*span, lookup((0, 3)), 0, unroll=True)
+    coefficients((0, 2), *outer)
+    sweep(va, vb, *outer, tiles=(0, 2))
     sweep(vb, va, (2, 6), (10, 14))
     sweep(va, vb, (3, 7), (9, 13))
     basis = vb
@@ -365,7 +376,7 @@
     )
     pl.semaphore_wait(news, len(known))
 
-    def exchange(src, slots, send, recv, axis):
+    def exchange(src, slots, send, recv, axis, earlier):
         me = gx if axis == 0 else gy
         size = DX if axis == 0 else DY
         for d in range(1, size):
@@ -375,6 +386,8 @@
                 device_id=to, device_id_type=MESH,
             ).start()
         slots[me] = src[...]
+        for copy in earlier:
+            copy.wait_send() if axis == 0 else copy.wait()
         arrived = slots.at[pl.ds(0, size - 1)]
         pltpu.make_async_copy(arrived, arrived, recv).wait()
         return pltpu.make_async_copy(arrived, arrived, send)
@@ -384,9 +397,9 @@
             items = [a + b for a, b in zip(items[::2], items[1::2])] + (items[-1:] if len(items) % 2 else [])
         return items[0]
 
-    sent_x = exchange(mine, stage1, xsend, xrecv, 0)
+    sent_x = exchange(mine, stage1, xsend, xrecv, 0, copies)
     half[...] = tree([stage1[n] for n in range(DX)])
-    sent_y = exchange(half, stage2, ysend, yrecv, 1)
+    sent_y = exchange(half, stage2, ysend, yrecv, 1, [sent_x])
 
     pa, pb, pc = [tree([stage2[n] for n in range(*ends)]) for ends in ((0, 6), (6, 10), (10, 16))]
     slot = lane % 16
@@ -574,10 +587,6 @@
 
         lax.fori_loop(HX - 1, HX + TX + 1, prolong, 0, unroll=5)
 
-    for copy in copies:
-        copy.wait_send()
-    sent_x.wait()
-    sent_y.wait()
 
     def finish(x, _):
         for t in range(2):
@@ -593,6 +602,7 @@
         return 0
 
     lax.fori_loop(HX, HX + TX, finish, 0, unroll=True)
+    sent_y.wait()
 
 
 def per_device(facies, source, facies_perm, facies_store, well_x, well_y, well_rate):

time: 35.7 us -> 35.6 us (level)
  no operation moved by 1% of the time
where the time goes in v6:
time: 35.6 us; the launch traced here: 35.4 us
  Pallas kernels  32.4 us (91%)
  local copies, waits for them, and re-layouts  3.01 us (8%)
    pallas_call x1, Pallas kernels, per_device(): pl.pallas_call(kernel, out_shape=jax.ShapeDtypeStruct((TX, TY, CELLS_Z),...  32.4 us
    unnamed x15, local copies, waits for them, and re-layouts  3.01 us

profile of v6, /device:TPU:1, one launch (start us, length us, event | category | flops | bytes accessed | tf_op | source)
XLA Modules:
  0.0 35.4 jit_solution(3643015100551322391)
XLA Ops:
  0.0 0.0 copy-start.5
  0.0 0.0 copy-start.6
  0.0 0.0 copy-start.2
  0.0 0.0 copy-start.3
  0.0 0.0 copy-start.4
  0.0 0.6 %copy-done.5 = s32[64]{0:T(128)S(1)} copy-done((s32[64]{0:T(128)S(1)}, s32[64]{0:T(128)}, u32[]{:S(2)}) %copy-start.5) | copy-done | bytes 280
  0.7 0.0 copy-done.6
  0.7 0.0 copy-done.2
  0.7 0.0 copy-done.3
  0.7 0.0 copy-done.4
  0.7 0.0 copy-start
  0.7 0.8 %copy-done = s32[8,16,128]{2,1,0:T(8,128)S(1)} copy-done((s32[8,16,128]{2,1,0:T(8,128)S(1)}, s32[8,16,128]{2,1,0:T(8,128)}, u32[]{:S(2)}) %copy-start) | copy-done | bytes 65560
  1.6 0.0 copy-start.1
  1.6 0.8 %copy-done.1 = f32[8,16,128]{2,1,0:T(8,128)S(1)} copy-done((f32[8,16,128]{2,1,0:T(8,128)S(1)}, f32[8,16,128]{2,1,0:T(8,128)}, u32[]{:S(2)}) %copy-start.1) | copy-done | bytes 65560
  2.4 32.4 %shard_map.73 = f32[8,16,128]{2,1,0:T(8,128)S(1)} custom-call(s32[8,16,128]{2,1,0:T(8,128)S(1)} %copy-done, f32[8,16,128]{2,1,0:T(8,128)S(1)} %copy-done.1, f32[8]{0:T(128)S(1)} %copy-done.2, f32[8]{0:T(128)S(1)} %copy-done.3, s32[1,64]{1,0:T(1,128)S(1)} %bitcast.3, s32[1,64]{1,0:T(1,128)S(1)} %bitcast.4, f32[1,64]{1,0:T(1,128)S(1)} %bitcast.5), custom_call_target="tpu_custom_call" | custom-call | tf_op jit(solution)/shard_map/pallas_call | solution.py:614
  34.8 0.6 %copy.9 = f32[8,16,128]{2,1,0:T(8,128)} copy(f32[8,16,128]{2,1,0:T(8,128)S(1)} %shard_map.73) | data formatting | bytes 131072
Async XLA Ops:
  0.0 0.7 %copy-start.5 = (s32[64]{0:T(128)S(1)}, s32[64]{0:T(128)}, u32[]{:S(2)}) copy-start(s32[64]{0:T(128)} %param.12) | copy-start | bytes 772
  0.0 0.7 %copy-start.6 = (f32[64]{0:T(128)S(1)}, f32[64]{0:T(128)}, u32[]{:S(2)}) copy-start(f32[64]{0:T(128)} %param.13) | copy-start | bytes 772
  0.0 0.7 %copy-start.2 = (f32[8]{0:T(128)S(1)}, f32[8]{0:T(128)}, u32[]{:S(2)}) copy-start(f32[8]{0:T(128)} %perm_ref.1) | copy-start | bytes 100
  0.0 0.7 %copy-start.3 = (f32[8]{0:T(128)S(1)}, f32[8]{0:T(128)}, u32[]{:S(2)}) copy-start(f32[8]{0:T(128)} %store_ref.1) | copy-start | bytes 100
  0.0 0.7 %copy-start.4 = (s32[64]{0:T(128)S(1)}, s32[64]{0:T(128)}, u32[]{:S(2)}) copy-start(s32[64]{0:T(128)} %param.11) | copy-start | bytes 772
  0.7 0.8 %copy-start = (s32[8,16,128]{2,1,0:T(8,128)S(1)}, s32[8,16,128]{2,1,0:T(8,128)}, u32[]{:S(2)}) copy-start(s32[8,16,128]{2,1,0:T(8,128)} %facies_hbm.1) | copy-start | bytes 196612
  1.6 0.8 %copy-start.1 = (f32[8,16,128]{2,1,0:T(8,128)S(1)}, f32[8,16,128]{2,1,0:T(8,128)}, u32[]{:S(2)}) copy-start(f32[8,16,128]{2,1,0:T(8,128)} %source_hbm.1) | copy-start | bytes 196612
